TPU v7x, 32 devices: a whole 2x2x4 slice. The times are simulated.
32 devices in a mesh: seq: 32 (over z, y, x, core), tp: 1.
Axes of the slice: x: 2, y: 2, z: 4, core: 2. Of those that a mesh axis runs over, the one named last changes fastest.
Arguments:
- hidden_in: bfloat16 [4, 2048, 4096], P(None, 'seq'), may hold values from -6 to 6
- ln_gain: float32 [4096], replicated, may hold values from 0.1 to 1.9
- ln_bias: float32 [4096], replicated, may hold values from -3 to 3
- w_qkv: bfloat16 [3, 4096, 4096], P(None, 'seq', 'tp'), may hold values from -0.09375 to 0.09375
- w_out: bfloat16 [4096, 4096], P('tp', 'seq'), may hold values from -1.5 to 1.5
- cache_kv: bfloat16 [4, 512, 2, 4096], P(None, 'seq', None, 'tp'), may hold values from -500 to 500
- cache_len: int32 [4], replicated, may hold values from 128 to 512, as said below
- owner: int32 [8192, 1], P('seq'), may hold values from 0 to 31; in each aligned block of 256 rows (0 to 255, 256 to 511, ...) at most 8 rows name the same one
Outputs:
- attn_out: bfloat16 [4, 2048, 4096], P(None, 'seq', 'tp')
- appended: bfloat16 [8192, 2, 4096], P('seq', None, 'tp')
Inputs may be any that keep to these rules, and one draw needn't show every extreme that they name: `cache_len`: at least 128; one request's cache holds exactly 512 positions. Among the 256 tokens of one device no owner is named more than 8 times.
All inputs are finite; a program needn't handle non-finite values.
Results may differ from a plain program's by a relative error of at most 0.013.
The roundings to bfloat16 on the way count: a program that leaves them out, or rounds other values in their place, can miss the bound.
Values may be sent and summed in bfloat16 or wider, within the bound.
No kernel may reach another device: no remote copies, remote signals or barrier semaphores. Data moves between devices by JAX's collectives and lax.ppermute only.
A program may use at most 512 MiB of HBM per device.

v0:
```python
import math

import jax
import jax.numpy as jnp
from jax import lax
from jax.sharding import PartitionSpec as P

HD = 256
ROT = 64
REQ = 4
SLOTS = 8


EPSILON = 1e-05
BASE_FREQ = 10000.0
MASKED = -1e30


def layer_norm(values_in, gain, shift):
    wide = values_in.astype(jnp.float32)
    center = jnp.mean(wide, axis=-1, keepdims=True)
    spread = wide - center
    variance = jnp.mean(spread * spread, axis=-1, keepdims=True)
    return (spread * lax.rsqrt(variance + EPSILON) * gain + shift).astype(jnp.bfloat16)


def rotate(heads_in, positions):
    pair_index = jnp.arange(ROT // 2).astype(jnp.float32)
    inverse = jnp.power(BASE_FREQ, -2.0 * pair_index / ROT)
    angles = positions.astype(jnp.float32)[:, None] * inverse[None, :]
    cosine = jnp.cos(angles)[:, None, :]
    sine = jnp.sin(angles)[:, None, :]
    leading = heads_in.shape[:-1]
    paired = heads_in[..., :ROT].reshape(leading + (ROT // 2, 2))
    even = paired[..., 0]
    odd = paired[..., 1]
    turned = jnp.stack([even * cosine - odd * sine, odd * cosine + even * sine], axis=-1).reshape(
        leading + (ROT,)
    )
    return jnp.concatenate([turned, heads_in[..., ROT:]], axis=-1)


def body(hidden_in, ln_gain, ln_bias, w_qkv, w_out, cache_kv, cache_len, owner):
    new_dev = hidden_in.shape[1]
    tok_rows = REQ * new_dev
    normed = layer_norm(hidden_in.reshape(tok_rows, hidden_in.shape[2]), ln_gain, ln_bias)
    width = w_qkv.shape[2]
    heads_here = width // HD
    seq_count = lax.axis_size("seq")
    seq_here = lax.axis_index("seq")
    cache_each = cache_kv.shape[1]
    cache_dev = REQ * cache_each
    cache_flat = cache_kv.reshape(cache_dev, 2, width)
    rows_dev = cache_dev + tok_rows
    request_ids = jnp.arange(REQ)
    projected = jnp.einsum(
        "tc,icw->itw",
        normed,
        lax.all_gather(w_qkv, "seq", axis=1, tiled=True),
        preferred_element_type=jnp.float32,
    )

    def length_of(requests):
        return jnp.sum(
            jnp.where(requests[:, None] == request_ids[None, :], cache_len[None, :], 0), axis=1
        )

    local_ids = jnp.arange(tok_rows)
    query_req = local_ids // new_dev
    query_pos = length_of(query_req) + seq_here * new_dev + local_ids % new_dev
    shape_heads = (tok_rows, heads_here, HD)
    query = rotate(projected[0].reshape(shape_heads), query_pos).astype(jnp.bfloat16)
    keys_new = (
        rotate(projected[1].reshape(shape_heads), query_pos)
        .astype(jnp.bfloat16)
        .reshape(tok_rows, width)
    )
    values_new = projected[2].astype(jnp.bfloat16)
    fresh = jnp.stack([keys_new, values_new], axis=1)
    local_rows = jnp.concatenate([cache_flat, fresh], axis=0)
    scale_factor = 1.0 / math.sqrt(HD)
    block_rows = lax.all_gather(local_rows, "seq", axis=0, tiled=True)
    highest = jnp.full((heads_here, tok_rows), MASKED, jnp.float32)
    count = block_rows.shape[0]
    row_ids = jnp.arange(count)
    source = jnp.floor_divide(row_ids, rows_dev)
    within = row_ids - source * rows_dev
    in_cache = within < cache_dev
    cache_req = jnp.floor_divide(within, cache_each)
    cache_slot = source * cache_each + within - cache_req * cache_each
    new_local = within - cache_dev
    new_req = jnp.floor_divide(new_local, new_dev)
    key_req = jnp.where(in_cache, cache_req, new_req)
    key_len = length_of(key_req)
    key_pos = jnp.where(
        in_cache, cache_slot, key_len + source * new_dev + new_local - new_req * new_dev
    )
    usable = jnp.logical_or(jnp.logical_not(in_cache), cache_slot < key_len)
    allowed = (
        usable[None, :]
        & (key_req[None, :] == query_req[:, None])
        & (key_pos[None, :] <= query_pos[:, None])
    )
    key_rows = block_rows[:, 0].reshape(count, heads_here, HD)
    value_rows = block_rows[:, 1].reshape(count, heads_here, HD)
    scores = (
        jnp.einsum("qhd,khd->hqk", query, key_rows, preferred_element_type=jnp.float32)
        * scale_factor
    )
    scores = jnp.where(allowed[None], scores, MASKED)
    raised = jnp.maximum(highest, jnp.max(scores, axis=-1))
    weights = jnp.where(allowed[None], jnp.exp(scores - raised[:, :, None]), 0.0)
    weight_sum = jnp.sum(weights, axis=-1)
    weighted = jnp.einsum(
        "hqk,khd->qhd", weights.astype(jnp.bfloat16), value_rows, preferred_element_type=jnp.float32
    )
    highest, weight_sum, weighted = (raised, weight_sum, weighted)
    attended = (
        (weighted / jnp.transpose(weight_sum)[:, :, None])
        .astype(jnp.bfloat16)
        .reshape(tok_rows, width)
    )
    partial_out = jnp.dot(
        attended,
        lax.all_gather(w_out, "seq", axis=1, tiled=True),
        preferred_element_type=jnp.float32,
    ).astype(jnp.bfloat16)
    summed = (
        lax.psum_scatter(partial_out, "tp", scatter_dimension=1, tiled=True)
        .astype(jnp.float32)
        .astype(jnp.bfloat16)
    )
    attn_out = summed.reshape(REQ, new_dev, summed.shape[1])
    owners = owner[:, 0]
    targets = jnp.arange(seq_count)
    marks = (owners[:, None] == targets[None, :]).astype(jnp.int32)
    earlier = jnp.cumsum(marks, axis=0) - marks
    slot_ids = owners * SLOTS + jnp.sum(earlier * marks, axis=1)
    placing = (jnp.arange(seq_count * SLOTS)[:, None] == slot_ids[None, :]).astype(jnp.bfloat16)
    outgoing = jnp.einsum("st,tkw->skw", placing, fresh, preferred_element_type=jnp.float32).astype(
        jnp.bfloat16
    )
    outgoing = outgoing.reshape(seq_count, SLOTS, 2, width)
    arrived = lax.all_to_all(outgoing, "seq", split_axis=0, concat_axis=0, tiled=True)
    appended = arrived.reshape(seq_count * SLOTS, 2, width)
    return (attn_out, appended)


def solution(mesh):
    return jax.shard_map(
        body,
        mesh=mesh,
        in_specs=(
            P(None, "seq", None),
            P(),
            P(),
            P(None, "seq", "tp"),
            P("tp", "seq"),
            P(None, "seq", None, "tp"),
            P(),
            P("seq", None),
        ),
        out_specs=(P(None, "seq", "tp"), P("seq", None, "tp")),
        check_vma=False,
    )
```

profile of v0, /device:TPU:17, one launch (start us, length us, event | category | flops | bytes accessed | tf_op | source)
XLA Modules:
  0.0 2079.6 jit_solution(1797335068735394851)
XLA Ops:
  14.3 514.1 %all-gather.4.cloned.1.call-done = bf16[3,4096,4096]{2,1,0:T(8,128)(2,1)} async-done(((bf16[3,128,4096]{2,1,0:T(8,128)(2,1)}), bf16[3,4096,4096]{2,1,0:T(8,128)(2,1)}) %all-gather.4.cloned.1.call-update) | async-done | bytes 100663312 | tf_op jit(solution)/shard_map/all_gather | solution.py:59
  528.4 41.3 %convolution_bitcast_fusion = f32[3,256,4096]{2,1,0:T(8,128)} fusion(bf16[3,4096,4096]{2,1,0:T(8,128)(2,1)} %all-gather.4.cloned.1.call-done, bf16[256,4096]{1,0:T(8,128)(2,1)} %fusion.16), kind=kOutput, calls=%fused_computation.10 | convolution fusion | flops 25769803776 | bytes 115343360 | tf_op jit(solution)/shard_map/tc,icw->itw/dot_general | solution.py:56
  569.7 2.5 fusion.19
  572.2 4.0 fusion.52
  586.9 2.9 copy.66
  589.8 3.8 copy.65
  598.3 4.2 pad_maximum_fusion
  602.5 4.2 convert_element_type.80
  606.7 4.4 maximum_maximum_fusion
  612.9 2.9 fusion.8
  618.0 5.5 all-to-all-start
  624.6 4.3 compare_and_fusion
  628.9 3.0 slice.74
  635.5 176.6 %all-to-all-done = bf16[32,8,2,4096]{3,1,2,0:T(8,128)(2,1)} async-done(((bf16[32,8,2,4096]{3,1,2,0:T(8,128)(2,1)}), bf16[32,8,2,4096]{3,1,2,0:T(8,128)(2,1)}, u32[]{:S(2)}, u32[]{:S(2)}) %all-to-all-start) | async-done | bytes 4194336 | tf_op jit(solution)/shard_map/all_to_all | solution.py:144
  812.2 2.5 copy.81
  814.6 6.4 copy.63
  821.0 714.8 %all-gather.6.cloned.1.call-done = bf16[10240,2,4096]{2,0,1:T(8,128)(2,1)} async-done(((bf16[320,2,4096]{2,0,1:T(8,128)(2,1)}), bf16[10240,2,4096]{2,0,1:T(8,128)(2,1)}) %all-gather.6.cloned.1.call-update) | async-done | bytes 167772176 | tf_op jit(solution)/shard_map/all_gather | solution.py:82
  1535.9 110.0 %fusion.51 = (bf16[10240,1,4096]{2,0,1:T(8,128)(2,1)}, bf16[10240,1,4096]{2,0,1:T(8,128)(2,1)}) fusion(bf16[10240,2,4096]{2,0,1:T(8,128)(2,1)} %all-gather.6.cloned.1.call-done), kind=kLoop, calls=%fused_computation.108 | loop fusion | bytes 335544320 | tf_op jit(solution)/shard_map/slice | solution.py:104
  1645.9 97.2 %copy.64 = bf16[10240,1,4096]{0,2,1:T(8,128)(2,1)} copy(bf16[10240,1,4096]{2,0,1:T(8,128)(2,1)} %get-tuple-element.9) | data formatting | bytes 167772160 | tf_op jit(solution)/shard_map/reshape;squeeze | solution.py:105
  1743.1 55.2 %copy.71 = bf16[1280,8,16,256]{3,2,1,0:T(8,128)(2,1)} copy(bf16[1280,8,16,256]{3,1,2,0:T(8,128)(2,1)} %bitcast.30) | data formatting | bytes 167772160
  1798.4 121.2 %fusion = (f32[16,256]{1,0:T(8,128)S(1)}, f32[16,256,10240]{2,1,0:T(8,128)}) fusion(pred[256,10240]{1,0:T(8,128)(4,1)S(1)} %copy-done.2, bf16[10240,16,256]{2,1,0:T(8,128)(2,1)} %bitcast.31, bf16[256,16,192]{2,0,1:T(8,128)(2,1)} %copy.77, bf16[256,16,64]{2,0,1:T(8,128)(2,1)} %copy.57), kind=kOutput, calls=%fused_computation.2 | convolution fusion | flops 21604855808 | bytes 256393216 | tf_op jit(solution)/shard_map/qhd,khd->hqk/dot_general | solution.py:107
  1919.6 56.6 %fusion.1 = f32[16,256]{1,0:T(8,128)S(1)} fusion(f32[16,256,10240]{2,1,0:T(8,128)} %get-tuple-element.21, f32[16,256]{1,0:T(8,128)S(1)} %broadcast_maximum_fusion, pred[256,10240]{1,0:T(8,128)(4,1)S(1)} %copy-done.2), kind=kLoop, calls=%fused_computation.3 | loop fusion | flops 209711104 | bytes 170426368 | tf_op jit(solution)/shard_map/reduce_sum | solution.py:113
  1976.2 79.9 %fusion.12 = bf16[256,16,256]{0,2,1:T(8,128)(2,1)} fusion(bf16[10240,16,256]{0,2,1:T(8,128)(2,1)} %bitcast.7, f32[16,256,10240]{2,1,0:T(8,128)} %get-tuple-element.21, f32[16,256]{1,0:T(8,128)S(1)} %broadcast_maximum_fusion, pred[256,10240]{1,0:T(8,128)(4,1)S(1)} %copy-done.2, f32[256,16]{0,1:T(8,128)S(1)} %bitcast.89), kind=kOutput, calls=%fused_computation.22 | convolution fusion | flops 21686648832 | bytes 256409600 | tf_op jit(solution)/shard_map/hqk,khd->qhd/dot_general | solution.py:114
  2056.0 16.6 convolution_convert_fusion.1
  (63 shorter events, 31.1 us)
Async XLA Ops:
  7.2 1.6 copy-start
  7.2 2.8 copy-start.5
  7.2 521.2 %all-gather.4.cloned.1.call-start = ((), (), s32[]{:S(2)}) async-start(), calls=%async_computation.1 | async-start | bytes 103809024 | tf_op jit(solution)/shard_map/all_gather | solution.py:59
  7.2 4.4 copy-start.9
  7.2 4.7 copy-start.6
  7.2 4.7 copy-start.7
  7.9 1527.9 %all-gather.6.cloned.1.call-start = ((), (), s32[]{:S(2)}) async-start(), calls=%async_computation.2 | async-start | bytes 173015040 | tf_op jit(solution)/shard_map/all_gather | solution.py:82
  583.3 2.0 copy-start.1
  598.3 8.4 copy-start.3
  611.1 0.7 copy-start.8
  618.0 194.2 %all-to-all-start = ((bf16[32,8,2,4096]{3,1,2,0:T(8,128)(2,1)}), bf16[32,8,2,4096]{3,1,2,0:T(8,128)(2,1)}, u32[]{:S(2)}, u32[]{:S(2)}) async-start(bf16[32,8,2,4096]{3,1,2,0:T(8,128)(2,1)} %copy.61), calls=%async_computation | async-start | bytes 8388608 | tf_op jit(solution)/shard_map/all_to_all | solution.py:144
  623.5 1432.5 %all-gather.8.cloned.1.call-start = ((), (), s32[]{:S(2)}) async-start(), calls=%async_computation.3 | async-start | bytes 34603008 | tf_op jit(solution)/shard_map/all_gather | solution.py:125
  628.9 5.0 copy-start.4
  1743.1 55.3 %copy-start.2 = (pred[256,10240]{1,0:T(8,128)(4,1)S(1)}, pred[256,10240]{1,0:T(8,128)(4,1)}, u32[]{:S(2)}) copy-start(pred[256,10240]{1,0:T(8,128)(4,1)} %compare_and_fusion) | copy-start | bytes 7864324
Sparse Core Ops, SparseCore 0:
  10.9 517.4 all-gather.3
  611.2 924.5 all-gather.5
  1537.4 192.3 all-gather.7
where the time goes:
time: 2090 us; the launch traced here: 2080 us
  waiting for transfers between devices  1410 us (67%)
  local copies, waits for them, and re-layouts  314 us (15%)
  matrix products  262 us (13%)
  other arithmetic  76.9 us (4%)
    all_gather x1, waiting for transfers between devices, body(): block_rows = lax.all_gather(local_rows, 'seq', axis=0, tiled=True)  715 us
    all_gather x1, waiting for transfers between devices, body(): lax.all_gather(w_qkv, 'seq', axis=1, tiled=True)  514 us
    all_to_all x1, waiting for transfers between devices, body(): lax.all_to_all(outgoing, 'seq', split_axis=0, concat_axis=0, tiled=True)  177 us
    dot_general x1, matrix products, body(): jnp.einsum('qhd,khd->hqk', query, key_rows, preferred_element_type=jnp.fl...  121 us
    slice x1, local copies, waits for them, and re-layouts, body(): key_rows = block_rows[:, 0].reshape(count, heads_here, HD)  110 us
    another operation x1, local copies, waits for them, and re-layouts, body(): value_rows = block_rows[:, 1].reshape(count, heads_here, HD)  97.2 us
    dot_general x1, matrix products, body(): jnp.einsum('hqk,khd->qhd', weights.astype(jnp.bfloat16), value_rows, pref...  79.9 us
    unnamed x28, local copies, waits for them, and re-layouts  78.9 us
  transfers between devices with their start and end apart: 4, of which 3 were waited for; matrix products, arithmetic and copies ran while one was open for 27% of the time, Pallas kernels for 0%

commit v1 on v0

--- a/solution.py
+++ b/solution.py
@@ -1,19 +1,24 @@
+import functools
 import math
 
 import jax
 import jax.numpy as jnp
 from jax import lax
+from jax.experimental import pallas as pl
+from jax.experimental.pallas import tpu as pltpu
+from jax.sharding import Mesh
 from jax.sharding import PartitionSpec as P
 
 HD = 256
 ROT = 64
 REQ = 4
 SLOTS = 8
-
+CORES = 2
 
 EPSILON = 1e-05
 BASE_FREQ = 10000.0
 MASKED = -1e30
+LANES = 128
 
 
 def layer_norm(values_in, gain, shift):
@@ -40,7 +45,289 @@
     return jnp.concatenate([turned, heads_in[..., ROT:]], axis=-1)
 
 
-def body(hidden_in, ln_gain, ln_bias, w_qkv, w_out, cache_kv, cache_len, owner):
+def rotary_tables(positions):
+    lane = jnp.arange(LANES)
+    pair_index = (lane // 2).astype(jnp.float32)
+    inverse = jnp.power(BASE_FREQ, -2.0 * pair_index / ROT)
+    angles = positions.astype(jnp.float32)[:, None] * inverse[None, :]
+    turned = lane < ROT
+    cosine = jnp.where(turned, jnp.cos(angles), 1.0)
+    sine = jnp.where(turned, jnp.where(lane % 2 == 0, -1.0, 1.0) * jnp.sin(angles), 0.0)
+    return cosine, sine
+
+
+def project_kernel(
+    place, x_ref, w0, w1, w2, w3, cos_ref, sin_ref, q_ref, k_ref, v_ref, send_ref, held, sem
+):
+    zs, rows_each = held.shape[1] // (REQ * CORES * w0.shape[2]), w0.shape[2]
+    width = held.shape[2]
+    here = place[0]
+
+    @pl.when(pl.program_id(0) == 0)
+    def _():
+        copies = []
+        for away, source in enumerate((w0, w1, w2, w3)):
+            chip = here ^ away
+            for z in range(zs):
+                for c in range(CORES):
+                    row = pl.multiple_of(((z * REQ + chip) * CORES + c) * rows_each, rows_each)
+                    for which in range(3):
+                        copies.append(
+                            pltpu.make_async_copy(
+                                source.at[z * CORES + c, which],
+                                held.at[which, pl.ds(row, rows_each)],
+                                sem.at[len(copies)],
+                            )
+                        )
+        for copy in copies:
+            copy.start()
+        for copy in copies:
+            copy.wait()
+
+    each = x_ref.shape[2]
+    rows = x_ref[...].reshape(CORES * REQ * each, x_ref.shape[3])
+    lane = lax.broadcasted_iota(jnp.int32, (each, LANES), 1)
+    even = lane % 2 == 0
+    for which in range(3):
+        out = jnp.dot(rows, held[which], preferred_element_type=jnp.float32)
+        for c in range(CORES):
+            for r in range(REQ):
+                start = (c * REQ + r) * each
+                part = out[start : start + each]
+                if which < 2:
+                    cosine, sine = cos_ref[0, r, c], sin_ref[0, r, c]
+                    pieces = []
+                    for head in range(width // HD):
+                        low = part[:, head * HD : head * HD + LANES]
+                        other = jnp.where(
+                            even, pltpu.roll(low, LANES - 1, 1), pltpu.roll(low, 1, 1)
+                        )
+                        pieces.append(low * cosine + other * sine)
+                        pieces.append(part[:, head * HD + LANES : (head + 1) * HD])
+                    part = jnp.concatenate(pieces, axis=1)
+                part = part.astype(jnp.bfloat16)
+                if which == 0:
+                    q_ref[0, r, c] = part
+                elif which == 1:
+                    k_ref[0, r, c] = part
+                    send_ref[r, 0, c, :, :width] = part
+                else:
+                    v_ref[0, r, c] = part
+                    send_ref[r, 0, c, :, width:] = part
+
+
+def project(x_all, weights, cosine, sine, chip):
+    zs = x_all.shape[0] // CORES
+    each, depth = x_all.shape[2], x_all.shape[3]
+    rows_each, width = weights[0].shape[2], weights[0].shape[3]
+    table = pl.BlockSpec((1, REQ, CORES, each, LANES), lambda z, s: (z, 0, 0, 0, 0))
+    token = pl.BlockSpec((1, REQ, CORES, each, width), lambda z, s: (z, 0, 0, 0, 0))
+    by_token = jax.ShapeDtypeStruct((zs, REQ, CORES, each, width), jnp.bfloat16)
+    return pl.pallas_call(
+        project_kernel,
+        grid_spec=pltpu.PrefetchScalarGridSpec(
+            num_scalar_prefetch=1,
+            grid=(zs,),
+            in_specs=[pl.BlockSpec((CORES, REQ, each, depth), lambda z, s: (z, 0, 0, 0))]
+            + [pl.BlockSpec(memory_space=pl.ANY)] * 4
+            + [table, table],
+            out_specs=[
+                token,
+                token,
+                token,
+                pl.BlockSpec((REQ, 1, CORES, each, 2 * width), lambda z, s: (0, z, 0, 0, 0)),
+            ],
+            scratch_shapes=[
+                pltpu.VMEM((3, depth, width), jnp.bfloat16),
+                pltpu.SemaphoreType.DMA((4 * zs * CORES * 3,)),
+            ],
+        ),
+        out_shape=[
+            by_token,
+            by_token,
+            by_token,
+            jax.ShapeDtypeStruct((REQ, zs, CORES, each, 2 * width), jnp.bfloat16),
+        ],
+        compiler_params=pltpu.CompilerParams(
+            vmem_limit_bytes=56 * 2**20, dimension_semantics=("arbitrary",)
+        ),
+        cost_estimate=pl.CostEstimate(
+            flops=2 * zs * CORES * REQ * each * depth * 3 * width,
+            bytes_accessed=2 * (x_all.size + 3 * depth * width * 2),
+            transcendentals=0,
+        ),
+    )(jnp.reshape(chip, (1,)).astype(jnp.int32), x_all, *weights, cosine, sine)
+
+
+def attend_kernel(length, q_ref, k_ref, v_ref, kc_ref, vc_ref, o_ref, *, blocks):
+    step = pl.program_id(1)
+    size = q_ref.shape[0]
+    factor = math.log2(math.e) / math.sqrt(HD)
+    contract = (((1,), (1,)), ((), ()))
+    slots = kc_ref.shape[0] * kc_ref.shape[1]
+
+    for index in range(blocks):
+
+        @pl.when(step == index)
+        def _(index=index):
+            query = q_ref[...]
+            k_old = kc_ref[...].reshape(slots, HD)
+            v_old = vc_ref[...].reshape(slots, HD)
+            old = lax.dot_general(query, k_old, contract, preferred_element_type=jnp.float32)
+            slot = lax.broadcasted_iota(jnp.int32, old.shape, 1)
+            old = jnp.where(slot < length[0], old, MASKED)
+            parts = [(old, v_old)]
+            if index:
+                span = index * size
+                parts.append(
+                    (
+                        lax.dot_general(
+                            query, k_ref[:span], contract, preferred_element_type=jnp.float32
+                        ),
+                        v_ref[:span],
+                    )
+                )
+            own = lax.dot_general(
+                query,
+                k_ref[index * size : (index + 1) * size],
+                contract,
+                preferred_element_type=jnp.float32,
+            )
+            row = lax.broadcasted_iota(jnp.int32, own.shape, 0)
+            column = lax.broadcasted_iota(jnp.int32, own.shape, 1)
+            own = jnp.where(column <= row, own, MASKED)
+            parts.append((own, v_ref[index * size : (index + 1) * size]))
+            highest = functools.reduce(
+                jnp.maximum, [jnp.max(s, axis=1, keepdims=True) for s, _ in parts]
+            )
+            total, mixed = 0.0, 0.0
+            for scores, values in parts:
+                weights = jnp.exp2((scores - highest) * factor)
+                total = total + jnp.sum(weights, axis=1, keepdims=True)
+                mixed = mixed + jnp.dot(
+                    weights.astype(jnp.bfloat16), values, preferred_element_type=jnp.float32
+                )
+            o_ref[...] = (mixed / total).astype(jnp.bfloat16)
+
+
+def attend(query, keys, values, cached, length):
+    count, width = query.shape
+    heads, size = width // HD, min(256, count)
+    blocks = count // size
+    sources, _, each, _ = cached.shape
+
+    def old(which):
+        return pl.BlockSpec((sources, None, each, HD), lambda h, i, s: (0, which, 0, h))
+
+    return pl.pallas_call(
+        functools.partial(attend_kernel, blocks=blocks),
+        grid_spec=pltpu.PrefetchScalarGridSpec(
+            num_scalar_prefetch=1,
+            grid=(heads, blocks),
+            in_specs=[
+                pl.BlockSpec((size, HD), lambda h, i, s: (i, h)),
+                pl.BlockSpec((count, HD), lambda h, i, s: (0, h)),
+                pl.BlockSpec((count, HD), lambda h, i, s: (0, h)),
+                old(0),
+                old(1),
+            ],
+            out_specs=pl.BlockSpec((size, HD), lambda h, i, s: (i, h)),
+        ),
+        out_shape=jax.ShapeDtypeStruct((count, width), jnp.bfloat16),
+        compiler_params=pltpu.CompilerParams(
+            vmem_limit_bytes=48 * 2**20, dimension_semantics=("arbitrary", "arbitrary")
+        ),
+        cost_estimate=pl.CostEstimate(
+            flops=4 * count * (count // 2 + sources * each) * width,
+            bytes_accessed=2 * 4 * count * width,
+            transcendentals=count * (count // 2 + sources * each) * heads,
+        ),
+    )(jnp.reshape(length, (1,)), query, keys, values, cached, cached)
+
+
+def slots_of(owners, count):
+    marks = (owners[:, None] == jnp.arange(count)[None, :]).astype(jnp.int32)
+    earlier = jnp.cumsum(marks, axis=0) - marks
+    return owners * SLOTS + jnp.sum(earlier * marks, axis=1)
+
+
+def by_heads(hidden_in, ln_gain, ln_bias, w_qkv, w_out, cache_kv, cache_len, owner):
+    zs, seq_count = lax.axis_size("z"), lax.axis_size("z") * REQ * CORES
+    groups = zs * CORES
+    chip = lax.axis_index("r")
+    seq = ("z", "r", "c")
+    new_dev, depth = hidden_in.shape[1], hidden_in.shape[2]
+    width = w_qkv.shape[2]
+    cols = width // groups
+
+    w_cut = w_qkv.reshape(3, w_qkv.shape[1], groups, cols).transpose(2, 0, 1, 3)
+    w_own = lax.all_to_all(w_cut, ("z", "c"), split_axis=0, concat_axis=0, tiled=True)
+    swap_x = [(0, 1), (1, 0), (2, 3), (3, 2)]
+    swap_y = [(0, 2), (2, 0), (1, 3), (3, 1)]
+    w_x = lax.ppermute(w_own, "r", swap_x)
+    w_y = lax.ppermute(w_own, "r", swap_y)
+    half = groups // 2
+    w_d = jnp.concatenate(
+        [lax.ppermute(w_x[:half], "r", swap_y), lax.ppermute(w_y[half:], "r", swap_x)], axis=0
+    )
+
+    normed = layer_norm(hidden_in, ln_gain, ln_bias)
+    x_own = lax.all_to_all(normed, "r", split_axis=0, concat_axis=0, tiled=True)
+    x_all = lax.all_gather(x_own, ("z", "c"), axis=0, tiled=False)
+
+    cache_each = cache_kv.shape[1]
+    cut = cache_kv.reshape(REQ, cache_each, 2, zs, CORES, cols).transpose(3, 0, 4, 2, 1, 5)
+    cached = lax.all_to_all(
+        cut.reshape(seq_count, 2, cache_each, cols), seq, split_axis=0, concat_axis=0, tiled=True
+    )
+
+    w_out_all = lax.all_gather(w_out, seq, axis=1, tiled=True)
+
+    length = jnp.sum(jnp.where(jnp.arange(REQ) == chip, cache_len, 0))
+    new_len = seq_count * new_dev
+    cosine, sine = rotary_tables(length + jnp.arange(new_len))
+    shape = (zs, REQ, CORES, new_dev, LANES)
+    query, keys, values, fresh = project(
+        x_all.reshape(groups, REQ, new_dev, depth),
+        (w_own, w_x, w_y, w_d),
+        cosine.reshape(shape),
+        sine.reshape(shape),
+        chip,
+    )
+    flat = (new_len, cols)
+
+    whole = lax.all_to_all(fresh, "r", split_axis=0, concat_axis=0, tiled=True)
+    slot_ids = lax.all_gather(slots_of(owner[:, 0], seq_count), ("z", "c"), axis=0, tiled=False)
+    slot_ids = slot_ids.reshape(groups, REQ * new_dev)
+
+    attended = attend(
+        query.reshape(flat), keys.reshape(flat), values.reshape(flat), cached, length
+    )
+    back = lax.all_to_all(
+        attended.reshape(seq_count, new_dev, cols), seq, split_axis=0, concat_axis=0, tiled=True
+    )
+
+    rows = whole.reshape(REQ, groups, new_dev, 2 * cols).transpose(1, 0, 2, 3)
+    rows = rows.reshape(groups, REQ * new_dev, 2 * cols)
+    placing = (
+        jnp.arange(seq_count * SLOTS)[None, :, None] == slot_ids[:, None, :]
+    ).astype(jnp.bfloat16)
+    outgoing = jnp.einsum("gst,gtw->gsw", placing, rows, preferred_element_type=jnp.float32)
+    outgoing = outgoing.astype(jnp.bfloat16).reshape(groups, seq_count, SLOTS, 2 * cols)
+    arrived = lax.all_to_all(
+        outgoing.transpose(1, 0, 2, 3), seq, split_axis=0, concat_axis=0, tiled=True
+    )
+    appended = arrived.reshape(zs, REQ, CORES, zs, CORES, SLOTS, 2, cols)
+    appended = appended.transpose(3, 1, 4, 5, 6, 0, 2, 7).reshape(seq_count * SLOTS, 2, width)
+
+    rows_back = back.reshape(zs, REQ, CORES, new_dev, cols).transpose(1, 3, 0, 2, 4)
+    out = jnp.dot(
+        rows_back.reshape(REQ * new_dev, width), w_out_all, preferred_element_type=jnp.float32
+    ).astype(jnp.bfloat16)
+    return out.reshape(REQ, new_dev, out.shape[1]), appended
+
+
+def by_tokens(hidden_in, ln_gain, ln_bias, w_qkv, w_out, cache_kv, cache_len, owner):
     new_dev = hidden_in.shape[1]
     tok_rows = REQ * new_dev
     normed = layer_norm(hidden_in.reshape(tok_rows, hidden_in.shape[2]), ln_gain, ln_bias)
@@ -80,7 +367,6 @@
     local_rows = jnp.concatenate([cache_flat, fresh], axis=0)
     scale_factor = 1.0 / math.sqrt(HD)
     block_rows = lax.all_gather(local_rows, "seq", axis=0, tiled=True)
-    highest = jnp.full((heads_here, tok_rows), MASKED, jnp.float32)
     count = block_rows.shape[0]
     row_ids = jnp.arange(count)
     source = jnp.floor_divide(row_ids, rows_dev)
@@ -108,13 +394,12 @@
         * scale_factor
     )
     scores = jnp.where(allowed[None], scores, MASKED)
-    raised = jnp.maximum(highest, jnp.max(scores, axis=-1))
-    weights = jnp.where(allowed[None], jnp.exp(scores - raised[:, :, None]), 0.0)
+    highest = jnp.max(scores, axis=-1)
+    weights = jnp.where(allowed[None], jnp.exp(scores - highest[:, :, None]), 0.0)
     weight_sum = jnp.sum(weights, axis=-1)
     weighted = jnp.einsum(
         "hqk,khd->qhd", weights.astype(jnp.bfloat16), value_rows, preferred_element_type=jnp.float32
     )
-    highest, weight_sum, weighted = (raised, weight_sum, weighted)
     attended = (
         (weighted / jnp.transpose(weight_sum)[:, :, None])
         .astype(jnp.bfloat16)
@@ -131,11 +416,7 @@
         .astype(jnp.bfloat16)
     )
     attn_out = summed.reshape(REQ, new_dev, summed.shape[1])
-    owners = owner[:, 0]
-    targets = jnp.arange(seq_count)
-    marks = (owners[:, None] == targets[None, :]).astype(jnp.int32)
-    earlier = jnp.cumsum(marks, axis=0) - marks
-    slot_ids = owners * SLOTS + jnp.sum(earlier * marks, axis=1)
+    slot_ids = slots_of(owner[:, 0], seq_count)
     placing = (jnp.arange(seq_count * SLOTS)[:, None] == slot_ids[None, :]).astype(jnp.bfloat16)
     outgoing = jnp.einsum("st,tkw->skw", placing, fresh, preferred_element_type=jnp.float32).astype(
         jnp.bfloat16
@@ -147,19 +428,36 @@
 
 
 def solution(mesh):
-    return jax.shard_map(
-        body,
-        mesh=mesh,
-        in_specs=(
-            P(None, "seq", None),
-            P(),
-            P(),
-            P(None, "seq", "tp"),
-            P("tp", "seq"),
-            P(None, "seq", None, "tp"),
-            P(),
-            P("seq", None),
-        ),
-        out_specs=(P(None, "seq", "tp"), P("seq", None, "tp")),
-        check_vma=False,
-    )
+    seq_count, tp_count = mesh.shape["seq"], mesh.shape["tp"]
+    zs = seq_count // (REQ * CORES)
+
+    def call(*args):
+        heads_here = args[3].shape[2] // tp_count // HD
+        split = (
+            tp_count == 1
+            and zs * REQ * CORES == seq_count
+            and heads_here % max(zs * CORES, 1) == 0
+        )
+        if split:
+            body, seq, names = by_heads, ("z", "r", "c"), ("z", "r", "c", "tp")
+            grid = Mesh(mesh.devices.reshape(zs, REQ, CORES, tp_count), names)
+        else:
+            body, seq, grid = by_tokens, "seq", mesh
+        return jax.shard_map(
+            body,
+            mesh=grid,
+            in_specs=(
+                P(None, seq, None),
+                P(),
+                P(),
+                P(None, seq, "tp"),
+                P("tp", seq),
+                P(None, seq, None, "tp"),
+                P(),
+                P(seq, None),
+            ),
+            out_specs=(P(None, seq, "tp"), P(seq, None, "tp")),
+            check_vma=False,
+        )(*args)
+
+    return call

time: 2090 us -> 728 us (0.35)
  waiting for transfers between devices: 1410 us -> 188 us
  local copies, waits for them, and re-layouts: 314 us -> 40 us
  blocking collectives: 0 us -> 253 us
  matrix products: 262 us -> 17.9 us
  starting transfers between devices: 5.61 us -> 133 us
  other arithmetic: 76.9 us -> 15.3 us
  Pallas kernels: 0 us -> 61.6 us
    all_gather x3 -> x2, waiting for transfers between devices: 1230 us -> 0.01 us  [the longest x1 0.01 us: by_heads(): x_all = lax.all_gather(x_own, ('z', 'c'), axis=0, tiled=False)]
    dot_general x5 -> x2, matrix products: 262 us -> 17.9 us  [the longest x1 16.6 us: by_heads(): jnp.dot(rows_back.reshape(REQ * new_dev, width), w_out_all, preferred_ele...]
    all_to_all x0 -> x2, blocking collectives: none -> 185 us  [the longest x1 158 us: by_heads(): lax.all_to_all(w_cut, ('z', 'c'), split_axis=0, concat_axis=0, tiled=True)]
    slice x7 -> x3, local copies, waits for them, and re-layouts: 123 us -> 1.65 us  [the longest x1 1.37 us: by_heads(): w_y[half:]]
    all_to_all x1 -> x4, starting transfers between devices: 5.49 us -> 122 us  [the longest x1 62.3 us: by_heads(): lax.all_to_all(attended.reshape(seq_count, new_dev, cols), seq, split_axi...]
    another operation x2 -> x1, local copies, waits for them, and re-layouts: 97.2 us -> 0.01 us  [call(): jax.shard_map(body, mesh=grid, in_specs=(P(None, seq, None), P(), P(), P(...]
    ppermute x0 -> x4, waiting for transfers between devices: none -> 84.1 us  [the longest x1 67.1 us: by_heads(): w_x = lax.ppermute(w_own, 'r', swap_x)]
    unnamed x28 -> x22, local copies, waits for them, and re-layouts: 78.9 us -> 3.66 us
  transfers between devices with their start and end apart: 4 -> 10, of which waited for: 3 -> 5; matrix products, arithmetic and copies ran while one was open for 27% -> 7% of each run, Pallas kernels for 0% -> 9%
where the time goes in v1:
time: 728 us; the launch traced here: 723 us
  blocking collectives  253 us (35%)
  waiting for transfers between devices  188 us (26%)
  starting transfers between devices  133 us (18%)
  Pallas kernels  61.6 us (8%)
  local copies, waits for them, and re-layouts  40 us (5%)
  matrix products  17.9 us (2%)
  other arithmetic  15.3 us (2%)
  between operations  14.3 us (2%)
    all_to_all x1, blocking collectives, by_heads(): lax.all_to_all(w_cut, ('z', 'c'), split_axis=0, concat_axis=0, tiled=True)  158 us
    all_to_all x1, waiting for transfers between devices, by_heads(): lax.all_to_all(outgoing.transpose(1, 0, 2, 3), seq, split_axis=0, concat_...  84.1 us
    all_gather x1, blocking collectives, by_heads(): lax.all_gather(slots_of(owner[:, 0], seq_count), ('z', 'c'), axis=0, tile...  67.8 us
    ppermute x1, waiting for transfers between devices, by_heads(): w_x = lax.ppermute(w_own, 'r', swap_x)  67.1 us
    all_to_all x1, starting transfers between devices, by_heads(): lax.all_to_all(attended.reshape(seq_count, new_dev, cols), seq, split_axi...  62.3 us
    all_to_all x1, starting transfers between devices, by_heads(): whole = lax.all_to_all(fresh, 'r', split_axis=0, concat_axis=0, tiled=True)  38.7 us
    pallas_call x1, Pallas kernels, project(): pl.pallas_call(project_kernel, grid_spec=pltpu.PrefetchScalarGridSpec(num...  36.3 us
    all_to_all x1, blocking collectives, by_heads(): x_own = lax.all_to_all(normed, 'r', split_axis=0, concat_axis=0, tiled=True)  27.7 us
  transfers between devices with their start and end apart: 10, of which 5 were waited for; matrix products, arithmetic and copies ran while one was open for 7% of the time, Pallas kernels for 9%

profile of v1, /device:TPU:17, one launch (start us, length us, event | category | flops | bytes accessed | tf_op | source)
XLA Modules:
  0.0 722.9 jit_solution(4402506721721022655)
XLA Ops:
  11.2 27.7 %all_to_all.30 = bf16[4,64,4096]{2,1,0:T(8,128)(2,1)} all-to-all(bf16[4,64,4096]{2,1,0:T(8,128)(2,1)S(1)} %fusion.5), channel_id=1, replica_groups=mesh['z'=4,'r'=4,'c'=2,'tp'=1] {'r'}, dimensions={0} | all-to-all | bytes 4194304 | tf_op jit(solution)/shard_map/all_to_all | solution.py:275
  39.7 2.8 copy.26
  42.4 3.2 copy.27
  45.6 157.6 %all_to_all.31.w0 = bf16[8,3,128,512]{3,2,1,0:T(8,128)(2,1)S(1)} all-to-all(bf16[8,3,128,512]{3,2,1,0:T(8,128)(2,1)S(1)} %bitcast.65), channel_id=1, replica_groups=mesh['z'=4,'r'=4,'c'=2,'tp'=1] {'z','c'}, dimensions={0} | all-to-all | bytes 6291456 | tf_op jit(solution)/shard_map/all_to_all | solution.py:264
  205.6 67.1 %collective-permute-done.w1 = bf16[8,3,128,512]{3,2,1,0:T(8,128)(2,1)S(1)} collective-permute-done((bf16[8,3,128,512]{3,2,1,0:T(8,128)(2,1)S(1)}, bf16[8,3,128,512]{3,2,1,0:T(8,128)(2,1)S(1)}, u32[]{:S(2)}, u32[]{:S(2)}) %collective-permute-start) | collective-permute-done | bytes 3145760 | tf_op jit(solution)/shard_map/ppermute | solution.py:267
  272.7 6.9 collective-permute-start.2
  286.9 12.3 %all-to-all-start.2 = ((bf16[32,2,16,512]{3,2,1,0:T(8,128)(2,1)}), bf16[32,2,16,512]{3,2,1,0:T(8,128)(2,1)S(1)}, u32[]{:S(2)}, u32[]{:S(2)}) async-start(bf16[32,2,16,512]{3,2,1,0:T(8,128)(2,1)} %bitcast.9), calls=%async_computation.2 | async-start | bytes 2097152 | tf_op jit(solution)/shard_map/all_to_all | solution.py:280
  300.4 5.7 fusion.8
  306.1 11.9 %collective-permute-done.2 = bf16[4,3,128,512]{3,2,1,0:T(8,128)(2,1)} collective-permute-done((bf16[4,3,128,512]{3,2,1,0:T(8,128)(2,1)S(1)}, bf16[4,3,128,512]{3,2,1,0:T(8,128)(2,1)}, u32[]{:S(2)}, u32[]{:S(2)}) %collective-permute-start.2) | collective-permute-done | bytes 1572896 | tf_op jit(solution)/shard_map/ppermute | solution.py:271
  318.0 5.2 collective-permute-done.3
  323.1 3.8 pad_maximum_fusion.w3
  326.9 36.3 %shard_map.95 = (bf16[4,4,2,64,512]{4,3,2,1,0:T(8,128)(2,1)}, bf16[4,4,2,64,512]{4,3,2,1,0:T(8,128)(2,1)}, bf16[4,4,2,64,512]{4,3,2,1,0:T(8,128)(2,1)}, bf16[4,4,2,64,1024]{4,3,2,1,0:T(8,128)(2,1)}) custom-call(s32[1]{0:T(128)} %bitcast.1.place, bf16[8,4,64,4096]{3,2,1,0:T(8,128)(2,1)} %bitcast.72, bf16[8,3,128,512]{3,2,1,0:T(8,128)(2,1)} %copy-done.3, ...), custom_call_target="tpu_custom_call" | custom-call | flops 25769803776 | bytes 41943040 | tf_op jit(solution)/shard_map/pallas_call | solution.py:126
  363.3 38.7 %all-to-all-start.4 = ((bf16[4,4,2,64,1024]{4,3,2,1,0:T(8,128)(2,1)}), bf16[4,4,2,64,1024]{4,3,2,1,0:T(8,128)(2,1)}, u32[]{:S(2)}, u32[]{:S(2)}) async-start(bf16[4,4,2,64,1024]{4,3,2,1,0:T(8,128)(2,1)} %get-tuple-element.9), calls=%async_computation.4 | async-start | bytes 8388608 | tf_op jit(solution)/shard_map/all_to_all | solution.py:299
  402.0 25.2 %shard_map.96 = bf16[2048,512]{1,0:T(8,128)(2,1)} custom-call(s32[1]{0:T(128)} %bitcast.length, bf16[2048,512]{1,0:T(8,128)(2,1)S(1)} %bitcast.62, bf16[2048,512]{1,0:T(8,128)(2,1)} %bitcast.73, bf16[2048,512]{1,0:T(8,128)(2,1)} %bitcast.74, bf16[32,2,16,512]{3,2,1,0:T(8,128)(2,1)S(1)} %all-to-all-done.2.kc_ref.vc_ref, ...), custom_call_target="tpu_custom_call" | custom-call | flops 6442450944 | bytes 8388608 | tf_op jit(solution)/shard_map/pallas_call | solution.py:222
  427.2 19.1 %all-to-all-done.4 = bf16[4,4,2,64,1024]{4,3,2,1,0:T(8,128)(2,1)} async-done(((bf16[4,4,2,64,1024]{4,3,2,1,0:T(8,128)(2,1)}), bf16[4,4,2,64,1024]{4,3,2,1,0:T(8,128)(2,1)}, u32[]{:S(2)}, u32[]{:S(2)}) %all-to-all-start.4) | async-done | bytes 4194336 | tf_op jit(solution)/shard_map/all_to_all | solution.py:299
  446.4 62.3 %all-to-all-start.3 = ((bf16[32,64,512]{2,1,0:T(8,128)(2,1)}), bf16[32,64,512]{2,1,0:T(8,128)(2,1)S(1)}, u32[]{:S(2)}, u32[]{:S(2)}) async-start(bf16[32,64,512]{2,1,0:T(8,128)(2,1)} %bitcast.10), calls=%async_computation.3 | async-start | bytes 4194304 | tf_op jit(solution)/shard_map/all_to_all | solution.py:306
  509.6 67.8 %all-gather.1 = s32[8,1,256]{2,1,0:T(1,128)S(1)} all-gather(s32[1,1,256]{2,1,0:T(1,128)S(1)} %fusion.14), channel_id=1, replica_groups=mesh['z'=4,'r'=4,'c'=2,'tp'=1] {'z','c'}, dimensions={0}, use_global_device_ids=true | all-gather | bytes 9216 | tf_op jit(solution)/shard_map/all_gather | solution.py:300
  583.7 8.6 %all-to-all-start.5 = ((bf16[32,8,8,1024]{3,2,1,0:T(8,128)(2,1)}), bf16[32,8,8,1024]{3,2,1,0:T(8,128)(2,1)}, u32[]{:S(2)}, u32[]{:S(2)}) async-start(bf16[32,8,8,1024]{3,2,1,0:T(8,128)(2,1)} %bitcast.64), calls=%async_computation.5 | async-start | bytes 8388608 | tf_op jit(solution)/shard_map/all_to_all | solution.py:317
  592.3 3.5 copy.29
  595.8 3.3 reshape.182
  599.1 84.1 %all-to-all-done.5 = bf16[32,8,8,1024]{3,2,1,0:T(8,128)(2,1)} async-done(((bf16[32,8,8,1024]{3,2,1,0:T(8,128)(2,1)}), bf16[32,8,8,1024]{3,2,1,0:T(8,128)(2,1)}, u32[]{:S(2)}, u32[]{:S(2)}) %all-to-all-start.5) | async-done | bytes 4194336 | tf_op jit(solution)/shard_map/all_to_all | solution.py:317
  683.2 8.6 %copy.33 = bf16[4,4,2,8,2,4,2,512]{7,6,5,4,3,2,1,0:T(2,128)(2,1)} copy(bf16[4,4,2,8,2,4,2,512]{7,3,4,2,0,6,1,5:T(8,128)(2,1)} %bitcast.26) | data formatting | bytes 8388608 | tf_op jit(solution)/shard_map/transpose | solution.py:321
  691.8 7.6 %reshape.189 = bf16[256,2,4096]{2,1,0:T(2,128)(2,1)} reshape(bf16[4,4,2,8,2,4,2,512]{7,6,5,4,3,2,1,0:T(2,128)(2,1)} %copy.33) | data formatting | bytes 8388608 | tf_op jit(solution)/shard_map/reshape | solution.py:321
  699.4 16.6 %convolution_convert_fusion = bf16[256,4096]{1,0:T(8,128)(2,1)} fusion(bf16[256,4096]{1,0:T(8,128)(2,1)S(1)} %reshape.182, bf16[4096,4096]{1,0:T(8,128)(2,1)} %all-gather.5.cloned.1.call-done), kind=kOutput, calls=%fused_computation.2 | convolution fusion | flops 8590983168 | bytes 37748736 | tf_op jit(solution)/shard_map/dot_general | solution.py:324
  (56 shorter events, 22.8 us)
Async XLA Ops:
  7.2 2.2 copy-start.1
  7.2 2.9 copy-start.6
  7.2 2.9 copy-start.7
  7.2 319.7 %all-gather.7.cloned.1.call-start = ((), (), s32[]{:S(2)}) async-start(), calls=%async_computation.7 | async-start | bytes 18874368 | tf_op jit(solution)/shard_map/all_gather | solution.py:276
  11.1 28.5 %copy-start.2 = (bf16[3,128,4096]{2,1,0:T(8,128)(2,1)S(1)}, bf16[3,128,4096]{2,1,0:T(8,128)(2,1)}, u32[]{:S(2)}) copy-start(bf16[3,128,4096]{2,1,0:T(8,128)(2,1)} %param.11) | copy-start | bytes 9437188
  38.9 660.5 %all-gather.5.cloned.1.call-start = ((), (), s32[]{:S(2)}) async-start(), calls=%async_computation.6 | async-start | bytes 34603008 | tf_op jit(solution)/shard_map/all_gather | solution.py:284
  203.2 77.8 %copy-start.3 = (bf16[8,3,128,512]{3,2,1,0:T(8,128)(2,1)}, bf16[8,3,128,512]{3,2,1,0:T(8,128)(2,1)S(1)}, u32[]{:S(2)}) copy-start(bf16[8,3,128,512]{3,2,1,0:T(8,128)(2,1)S(1)} %all_to_all.31.w0) | copy-start | bytes 9437188
  203.2 69.4 %collective-permute-start = (bf16[8,3,128,512]{3,2,1,0:T(8,128)(2,1)S(1)}, bf16[8,3,128,512]{3,2,1,0:T(8,128)(2,1)S(1)}, u32[]{:S(2)}, u32[]{:S(2)}) collective-permute-start(bf16[8,3,128,512]{3,2,1,0:T(8,128)(2,1)S(1)} %all_to_all.31.w0), channel_id=1, source_target_pairs={{0,2},{2,0},{4,6},{6,4},{1,3},{3,1},{5,7},{7,5},{8,10},{10,8},{12,... | collective-permute-start | bytes 9437192 | tf_op jit(solution)/shard_map/ppermute | solution.py:267
  204.4 75.3 %collective-permute-start.1 = (bf16[8,3,128,512]{3,2,1,0:T(8,128)(2,1)S(1)}, bf16[8,3,128,512]{3,2,1,0:T(8,128)(2,1)S(1)}, u32[]{:S(2)}, u32[]{:S(2)}) collective-permute-start(bf16[8,3,128,512]{3,2,1,0:T(8,128)(2,1)S(1)} %all_to_all.31.w0), channel_id=1, source_target_pairs={{0,4},{4,0},{2,6},{6,2},{1,5},{5,1},{3,7},{7,3},{8,12},{12,8},{10,... | collective-permute-start | bytes 9437192 | tf_op jit(solution)/shard_map/ppermute | solution.py:268
  272.6 8.4 %copy-start.4 = (bf16[8,3,128,512]{3,2,1,0:T(8,128)(2,1)}, bf16[8,3,128,512]{3,2,1,0:T(8,128)(2,1)S(1)}, u32[]{:S(2)}) copy-start(bf16[8,3,128,512]{3,2,1,0:T(8,128)(2,1)S(1)} %collective-permute-done.w1) | copy-start | bytes 9437188
  272.7 45.2 %collective-permute-start.2 = (bf16[4,3,128,512]{3,2,1,0:T(8,128)(2,1)S(1)}, bf16[4,3,128,512]{3,2,1,0:T(8,128)(2,1)}, u32[]{:S(2)}, u32[]{:S(2)}) collective-permute-start(bf16[4,3,128,512]{3,2,1,0:T(8,128)(2,1)S(1)} %slice.16), channel_id=1, source_target_pairs={{0,4},{4,0},{2,6},{6,2},{1,5},{5,1},{3,7},{7,3},{8,12},{12,8},{10,... | collective-permute-start | bytes 4718600 | tf_op jit(solution)/shard_map/ppermute | solution.py:271
  279.7 2.2 copy-start.5
  281.9 17.3 %copy-start.9 = (s32[4]{0:T(128)S(1)}, s32[4]{0:T(128)}, u32[]{:S(2)}) copy-start(s32[4]{0:T(128)} %param.14) | copy-start | bytes 52
  281.9 41.3 %collective-permute-start.3 = (bf16[4,3,128,512]{3,2,1,0:T(8,128)(2,1)}, bf16[4,3,128,512]{3,2,1,0:T(8,128)(2,1)}, u32[]{:S(2)}, u32[]{:S(2)}) collective-permute-start(bf16[4,3,128,512]{3,2,1,0:T(8,128)(2,1)} %slice.17), channel_id=1, source_target_pairs={{0,2},{2,0},{4,6},{6,4},{1,3},{3,1},{5,7},{7,5},{8,10},{10,8},{12,... | collective-permute-start | bytes 4718600 | tf_op jit(solution)/shard_map/ppermute | solution.py:271
  286.9 76.4 %all-to-all-start.2 = ((bf16[32,2,16,512]{3,2,1,0:T(8,128)(2,1)}), bf16[32,2,16,512]{3,2,1,0:T(8,128)(2,1)S(1)}, u32[]{:S(2)}, u32[]{:S(2)}) async-start(bf16[32,2,16,512]{3,2,1,0:T(8,128)(2,1)} %bitcast.9), calls=%async_computation.2 | async-start | bytes 2097152 | tf_op jit(solution)/shard_map/all_to_all | solution.py:280
  363.2 38.7 %copy-start = (bf16[4,4,2,64,512]{4,3,2,1,0:T(8,128)(2,1)S(1)}, bf16[4,4,2,64,512]{4,3,2,1,0:T(8,128)(2,1)}, u32[]{:S(2)}) copy-start(bf16[4,4,2,64,512]{4,3,2,1,0:T(8,128)(2,1)} %get-tuple-element.6) | copy-start | bytes 6291460
  363.3 83.1 %all-to-all-start.4 = ((bf16[4,4,2,64,1024]{4,3,2,1,0:T(8,128)(2,1)}), bf16[4,4,2,64,1024]{4,3,2,1,0:T(8,128)(2,1)}, u32[]{:S(2)}, u32[]{:S(2)}) async-start(bf16[4,4,2,64,1024]{4,3,2,1,0:T(8,128)(2,1)} %get-tuple-element.9), calls=%async_computation.4 | async-start | bytes 8388608 | tf_op jit(solution)/shard_map/all_to_all | solution.py:299
  427.2 81.4 %copy-start.8 = (s32[256,1]{0,1:T(1,128)S(1)}, s32[256,1]{0,1:T(1,128)}, u32[]{:S(2)}) copy-start(s32[256,1]{0,1:T(1,128)} %param.15) | copy-start | bytes 3076
  446.4 137.3 %all-to-all-start.3 = ((bf16[32,64,512]{2,1,0:T(8,128)(2,1)}), bf16[32,64,512]{2,1,0:T(8,128)(2,1)S(1)}, u32[]{:S(2)}, u32[]{:S(2)}) async-start(bf16[32,64,512]{2,1,0:T(8,128)(2,1)} %bitcast.10), calls=%async_computation.3 | async-start | bytes 4194304 | tf_op jit(solution)/shard_map/all_to_all | solution.py:306
  583.7 99.5 %all-to-all-start.5 = ((bf16[32,8,8,1024]{3,2,1,0:T(8,128)(2,1)}), bf16[32,8,8,1024]{3,2,1,0:T(8,128)(2,1)}, u32[]{:S(2)}, u32[]{:S(2)}) async-start(bf16[32,8,8,1024]{3,2,1,0:T(8,128)(2,1)} %bitcast.64), calls=%async_computation.5 | async-start | bytes 8388608 | tf_op jit(solution)/shard_map/all_to_all | solution.py:317
Sparse Core Ops, SparseCore 0:
  39.0 214.7 all-gather.6
  255.4 327.2 all-gather.4

commit v2 on v1

--- a/solution.py
+++ b/solution.py
@@ -14,6 +14,7 @@
 REQ = 4
 SLOTS = 8
 CORES = 2
+Z_CHIPS = 4
 
 EPSILON = 1e-05
 BASE_FREQ = 10000.0
@@ -56,107 +57,188 @@
     return cosine, sine
 
 
-def project_kernel(
-    place, x_ref, w0, w1, w2, w3, cos_ref, sin_ref, q_ref, k_ref, v_ref, send_ref, held, sem
-):
-    zs, rows_each = held.shape[1] // (REQ * CORES * w0.shape[2]), w0.shape[2]
-    width = held.shape[2]
-    here = place[0]
-
-    @pl.when(pl.program_id(0) == 0)
+def project_kernel(place, *refs):
+    q_ref, k_ref, v_ref, send_ref, rows_ref, held, sem_x, sem_w = refs[-8:]
+    steps, _, _, each, depth = rows_ref.shape
+    weights, (cos_ref, sin_ref) = refs[:10], refs[10:12]
+    sources = refs[12 : 12 + 2 * steps]
+    groups, _, rows_each, width = weights[0].shape
+    zs = groups // CORES
+    chip, core, step = place[0], place[1], pl.program_id(0)
+
+    def row_copy(index, c, away):
+        return pltpu.make_async_copy(
+            sources[2 * index + c].at[away],
+            rows_ref.at[index, core ^ c, chip ^ away],
+            sem_x.at[index, c, away],
+        )
+
+    def weight_copy(which, away, z, c):
+        row = pl.multiple_of(((z * REQ + (chip ^ away)) * CORES + c) * rows_each, rows_each)
+        group = z * CORES + c
+        piece = away + (away == 3 and group >= groups // 2)
+        inside = group - groups // 2 if piece == 4 else group
+        return pltpu.make_async_copy(
+            weights[5 * (which // 2) + piece].at[inside, which % 2],
+            held.at[which, pl.ds(row, rows_each)],
+            sem_w.at[which, away, group],
+        )
+
+    row_parts = [(c, away) for c in range(CORES) for away in range(REQ)]
+    weight_parts = [
+        (away, z, c) for away in range(REQ) for z in range(zs) for c in range(CORES)
+    ]
+
+    @pl.when(step == 0)
     def _():
-        copies = []
-        for away, source in enumerate((w0, w1, w2, w3)):
-            chip = here ^ away
-            for z in range(zs):
-                for c in range(CORES):
-                    row = pl.multiple_of(((z * REQ + chip) * CORES + c) * rows_each, rows_each)
-                    for which in range(3):
-                        copies.append(
-                            pltpu.make_async_copy(
-                                source.at[z * CORES + c, which],
-                                held.at[which, pl.ds(row, rows_each)],
-                                sem.at[len(copies)],
-                            )
-                        )
-        for copy in copies:
-            copy.start()
-        for copy in copies:
-            copy.wait()
-
-    each = x_ref.shape[2]
-    rows = x_ref[...].reshape(CORES * REQ * each, x_ref.shape[3])
-    lane = lax.broadcasted_iota(jnp.int32, (each, LANES), 1)
+        for part in row_parts:
+            row_copy(0, *part).start()
+        for part in weight_parts:
+            weight_copy(0, *part).start()
+
+    for index in range(steps):
+
+        @pl.when(step == index)
+        def _(index=index):
+            for part in row_parts:
+                row_copy(index, *part).wait()
+
+    count = CORES * REQ * each
+    lane = lax.broadcasted_iota(jnp.int32, (count, LANES), 1)
     even = lane % 2 == 0
+    cosine = cos_ref[...].reshape(count, LANES)
+    sine = sin_ref[...].reshape(count, LANES)
     for which in range(3):
+
+        @pl.when(step == 0)
+        def _(which=which):
+            for part in weight_parts:
+                weight_copy(which, *part).wait()
+            if which < 2:
+                for part in weight_parts:
+                    weight_copy(which + 1, *part).start()
+            else:
+                for index in range(1, steps):
+                    for part in row_parts:
+                        row_copy(index, *part).start()
+
+        rows = rows_ref[step].reshape(count, depth)
         out = jnp.dot(rows, held[which], preferred_element_type=jnp.float32)
+        if which < 2:
+            pieces = []
+            for head in range(width // HD):
+                low = out[:, head * HD : head * HD + LANES]
+                other = jnp.where(even, pltpu.roll(low, LANES - 1, 1), pltpu.roll(low, 1, 1))
+                pieces.append(low * cosine + other * sine)
+                pieces.append(out[:, head * HD + LANES : (head + 1) * HD])
+            out = jnp.concatenate(pieces, axis=1)
+        out = out.astype(jnp.bfloat16).reshape(CORES, REQ, each, width)
         for c in range(CORES):
             for r in range(REQ):
-                start = (c * REQ + r) * each
-                part = out[start : start + each]
-                if which < 2:
-                    cosine, sine = cos_ref[0, r, c], sin_ref[0, r, c]
-                    pieces = []
-                    for head in range(width // HD):
-                        low = part[:, head * HD : head * HD + LANES]
-                        other = jnp.where(
-                            even, pltpu.roll(low, LANES - 1, 1), pltpu.roll(low, 1, 1)
-                        )
-                        pieces.append(low * cosine + other * sine)
-                        pieces.append(part[:, head * HD + LANES : (head + 1) * HD])
-                    part = jnp.concatenate(pieces, axis=1)
-                part = part.astype(jnp.bfloat16)
+                part = out[c, r]
                 if which == 0:
                     q_ref[0, r, c] = part
                 elif which == 1:
                     k_ref[0, r, c] = part
-                    send_ref[r, 0, c, :, :width] = part
+                    send_ref[r ^ chip, 0, c, :, :width] = part
                 else:
                     v_ref[0, r, c] = part
-                    send_ref[r, 0, c, :, width:] = part
-
-
-def project(x_all, weights, cosine, sine, chip):
-    zs = x_all.shape[0] // CORES
-    each, depth = x_all.shape[2], x_all.shape[3]
-    rows_each, width = weights[0].shape[2], weights[0].shape[3]
-    table = pl.BlockSpec((1, REQ, CORES, each, LANES), lambda z, s: (z, 0, 0, 0, 0))
-    token = pl.BlockSpec((1, REQ, CORES, each, width), lambda z, s: (z, 0, 0, 0, 0))
-    by_token = jax.ShapeDtypeStruct((zs, REQ, CORES, each, width), jnp.bfloat16)
+                    send_ref[r ^ chip, 0, c, :, width:] = part
+
+
+def project(x_pairs, weights, cosine, sine, place, held, cost):
+    steps = len(x_pairs) // CORES
+    _, each, depth = x_pairs[0].shape
+    groups, _, rows_each, width = weights[0].shape
+    zs = groups // CORES
+    table = pl.BlockSpec((1, CORES, REQ, each, LANES), lambda i, s: (s[2 + i], 0, 0, 0, 0))
+    token = pl.BlockSpec((1, REQ, CORES, each, width), lambda i, s: (s[2 + i], 0, 0, 0, 0))
+    whole = jax.ShapeDtypeStruct((zs, REQ, CORES, each, width), jnp.bfloat16)
+    anywhere = pl.BlockSpec(memory_space=pl.ANY)
     return pl.pallas_call(
         project_kernel,
         grid_spec=pltpu.PrefetchScalarGridSpec(
             num_scalar_prefetch=1,
-            grid=(zs,),
-            in_specs=[pl.BlockSpec((CORES, REQ, each, depth), lambda z, s: (z, 0, 0, 0))]
-            + [pl.BlockSpec(memory_space=pl.ANY)] * 4
-            + [table, table],
+            grid=(steps,),
+            in_specs=[anywhere] * len(weights)
+            + [table, table]
+            + [anywhere] * (len(x_pairs) + len(held)),
             out_specs=[
                 token,
                 token,
                 token,
-                pl.BlockSpec((REQ, 1, CORES, each, 2 * width), lambda z, s: (0, z, 0, 0, 0)),
+                pl.BlockSpec(
+                    (REQ, 1, CORES, each, 2 * width), lambda i, s: (0, i, 0, 0, 0)
+                ),
             ],
             scratch_shapes=[
+                pltpu.VMEM((steps, CORES, REQ, each, depth), jnp.bfloat16),
                 pltpu.VMEM((3, depth, width), jnp.bfloat16),
-                pltpu.SemaphoreType.DMA((4 * zs * CORES * 3,)),
+                pltpu.SemaphoreType.DMA((steps, CORES, REQ)),
+                pltpu.SemaphoreType.DMA((3, REQ, groups)),
             ],
         ),
         out_shape=[
-            by_token,
-            by_token,
-            by_token,
-            jax.ShapeDtypeStruct((REQ, zs, CORES, each, 2 * width), jnp.bfloat16),
+            whole,
+            whole,
+            whole,
+            jax.ShapeDtypeStruct((REQ, steps, CORES, each, 2 * width), jnp.bfloat16),
         ],
+        input_output_aliases={3 + len(weights) + len(x_pairs) + i: i for i in range(len(held))},
+        compiler_params=pltpu.CompilerParams(
+            vmem_limit_bytes=58 * 2**20, dimension_semantics=("arbitrary",)
+        ),
+        cost_estimate=pl.CostEstimate(
+            flops=2 * steps * CORES * REQ * each * depth * 3 * width * cost,
+            bytes_accessed=2 * (x_pairs[0].size * len(x_pairs) + 3 * depth * width) * cost,
+            transcendentals=0,
+        ),
+    )(place, *weights, cosine, sine, *x_pairs, *held)
+
+
+def order_kernel(blocks, slot_ref, *refs):
+    out_ref = refs[-1]
+    owners = out_ref.shape[0]
+    count = slot_ref.shape[3]
+    wanted = lax.broadcasted_iota(jnp.int32, (owners * SLOTS, count), 0)
+    index = 0
+    for call in range(len(refs) // REQ):
+        parts = refs[call * REQ : (call + 1) * REQ]
+        for step in range(parts[0].shape[0]):
+            ordered = []
+            for c in range(CORES):
+                placing = (wanted == slot_ref[index, c]).astype(jnp.bfloat16)
+                rows = jnp.concatenate([part[step, c] for part in parts], axis=0)
+                out = jnp.dot(placing, rows, preferred_element_type=jnp.float32)
+                ordered.append(out.reshape(owners, SLOTS, rows.shape[1]))
+            both = jnp.concatenate(ordered, axis=1).astype(jnp.bfloat16)
+            out_ref[:, pl.ds(blocks[index], 1)] = both[:, None]
+            index += 1
+
+
+def order(blocks, slot_ids, parts, owners):
+    zs = slot_ids.shape[0]
+    each, wide = parts[0].shape[-2:]
+    out = (owners, zs, CORES * SLOTS, wide)
+    return pl.pallas_call(
+        order_kernel,
+        grid_spec=pltpu.PrefetchScalarGridSpec(
+            num_scalar_prefetch=1,
+            grid=(1,),
+            in_specs=[pl.BlockSpec(slot_ids.shape, lambda i, s: (0, 0, 0, 0))]
+            + [pl.BlockSpec(part.shape, lambda i, s: (0, 0, 0, 0)) for part in parts],
+            out_specs=pl.BlockSpec(out, lambda i, s: (0, 0, 0, 0)),
+        ),
+        out_shape=jax.ShapeDtypeStruct(out, jnp.bfloat16),
         compiler_params=pltpu.CompilerParams(
             vmem_limit_bytes=56 * 2**20, dimension_semantics=("arbitrary",)
         ),
         cost_estimate=pl.CostEstimate(
-            flops=2 * zs * CORES * REQ * each * depth * 3 * width,
-            bytes_accessed=2 * (x_all.size + 3 * depth * width * 2),
+            flops=2 * zs * CORES * (owners * SLOTS) * REQ * each * wide,
+            bytes_accessed=4 * owners * zs * CORES * SLOTS * wide,
             transcendentals=0,
         ),
-    )(jnp.reshape(chip, (1,)).astype(jnp.int32), x_all, *weights, cosine, sine)
+    )(blocks, slot_ids, *parts)
 
 
 def attend_kernel(length, q_ref, k_ref, v_ref, kc_ref, vc_ref, o_ref, *, blocks):
@@ -245,85 +327,299 @@
     )(jnp.reshape(length, (1,)), query, keys, values, cached, cached)
 
 
+def output_kernel(place, *refs):
+    mine_ref, other_ref, lhs, held, sem_l, sem_w = refs[-6:]
+    sources, weights = refs[:CORES], refs[CORES:-6]
+    zs = lhs.shape[3] // (sources[0].shape[2] * CORES)
+    each, cols = sources[0].shape[1:]
+    lanes = weights[0].shape[2]
+    depth = lhs.shape[3]
+    chip, step = place[0], pl.program_id(0)
+
+    def row_copy(which, z, r, c):
+        source = (z * REQ + r) * CORES + c
+        return pltpu.make_async_copy(
+            sources[which].at[source],
+            lhs.at[which, r, :, pl.ds((z * CORES + c) * cols, cols)],
+            sem_l.at[which, source],
+        )
+
+    row_parts = [
+        (which, z, r, c)
+        for which in range(CORES)
+        for z in range(zs)
+        for r in range(REQ)
+        for c in range(CORES)
+    ]
+
+    def weight_copies(index, r):
+        column = pl.multiple_of((chip ^ r) * lanes, lanes)
+        if index == 0:
+            pairs = [(weights[0].at[r], held.at[0, :, pl.ds(r * lanes, lanes)])]
+        elif index == 1:
+            half = depth // 2
+            pairs = [
+                (
+                    weights[4 + part].at[0] if r == 3 else weights[1 + r].at[part],
+                    held.at[1, pl.ds(part * half, half), pl.ds(column, lanes)],
+                )
+                for part in range(2)
+            ]
+        else:
+            part = index - 2
+            source = weights[9 + part].at[0] if r == 3 else weights[6 + r].at[part]
+            pairs = [(source, held.at[index, :, pl.ds(column, lanes)])]
+        return [
+            pltpu.make_async_copy(source, target, sem_w.at[index, r, number])
+            for number, (source, target) in enumerate(pairs)
+        ]
+
+    @pl.when(step == 0)
+    def _():
+        for part in row_parts:
+            row_copy(*part).start()
+        for index in range(zs):
+            for r in range(REQ):
+                for copy in weight_copies(index, r):
+                    copy.start()
+        for part in row_parts:
+            row_copy(*part).wait()
+
+    for index in range(zs):
+
+        @pl.when(step == index)
+        def _(index=index):
+            for r in range(REQ):
+                for copy in weight_copies(index, r):
+                    copy.wait()
+
+    rows = lhs[...].reshape(CORES * REQ * each, depth)
+    out = jnp.dot(rows, held[step], preferred_element_type=jnp.float32).astype(jnp.bfloat16)
+    mine_ref[...] = out[: REQ * each]
+    other_ref[...] = out[REQ * each :]
+
+
+def output(place, back, back_other, weights):
+    sources, each, cols = back.shape
+    _, depth, lanes = weights[0].shape
+    zs = sources // (REQ * CORES)
+    anywhere = pl.BlockSpec(memory_space=pl.ANY)
+    block = pl.BlockSpec((REQ * each, REQ * lanes), lambda i, s: (0, s[1 + i]))
+    shape = jax.ShapeDtypeStruct((REQ * each, zs * REQ * lanes), jnp.bfloat16)
+    return pl.pallas_call(
+        output_kernel,
+        grid_spec=pltpu.PrefetchScalarGridSpec(
+            num_scalar_prefetch=1,
+            grid=(zs,),
+            in_specs=[anywhere] * (CORES + len(weights)),
+            out_specs=[block, block],
+            scratch_shapes=[
+                pltpu.VMEM((CORES, REQ, each, depth), jnp.bfloat16),
+                pltpu.VMEM((zs, depth, REQ * lanes), jnp.bfloat16),
+                pltpu.SemaphoreType.DMA((CORES, sources)),
+                pltpu.SemaphoreType.DMA((zs, REQ, 2)),
+            ],
+        ),
+        out_shape=[shape, shape],
+        compiler_params=pltpu.CompilerParams(
+            vmem_limit_bytes=56 * 2**20, dimension_semantics=("arbitrary",)
+        ),
+        cost_estimate=pl.CostEstimate(
+            flops=2 * CORES * REQ * each * depth * zs * REQ * lanes,
+            bytes_accessed=2 * (2 * back.size + depth * zs * REQ * lanes),
+            transcendentals=0,
+        ),
+    )(place, back, back_other, *weights)
+
+
+def interleave_kernel(place, mine_ref, other_ref, out_ref):
+    lanes = LANES
+    core = place[0]
+    for block in range(mine_ref.shape[1] // lanes):
+        part = slice(block * lanes, (block + 1) * lanes)
+        here = pl.multiple_of((CORES * block + core) * lanes, lanes)
+        there = pl.multiple_of((CORES * block + 1 - core) * lanes, lanes)
+        out_ref[:, pl.ds(here, lanes)] = mine_ref[:, part]
+        out_ref[:, pl.ds(there, lanes)] = other_ref[:, part]
+
+
+def interleave(core, mine, other):
+    rows, width = mine.shape
+    tile = pl.BlockSpec((rows, width // 2), lambda i, s: (0, i))
+    return pl.pallas_call(
+        interleave_kernel,
+        grid_spec=pltpu.PrefetchScalarGridSpec(
+            num_scalar_prefetch=1,
+            grid=(2,),
+            in_specs=[tile, tile],
+            out_specs=pl.BlockSpec((rows, width), lambda i, s: (0, i)),
+        ),
+        out_shape=jax.ShapeDtypeStruct((rows, CORES * width), mine.dtype),
+        compiler_params=pltpu.CompilerParams(dimension_semantics=("arbitrary",)),
+        cost_estimate=pl.CostEstimate(
+            flops=0, bytes_accessed=8 * rows * width, transcendentals=0
+        ),
+    )(jnp.reshape(core, (1,)), mine, other)
+
+
 def slots_of(owners, count):
     marks = (owners[:, None] == jnp.arange(count)[None, :]).astype(jnp.int32)
     earlier = jnp.cumsum(marks, axis=0) - marks
     return owners * SLOTS + jnp.sum(earlier * marks, axis=1)
 
 
+def swap_chips(value, away):
+    return lax.ppermute(value, "r", [(chip, chip ^ away) for chip in range(REQ)])
+
+
+def swap_cores(value):
+    return lax.ppermute(value, "c", [(0, 1), (1, 0)])
+
+
+def z_step(up, down, step):
+    last = Z_CHIPS - 1
+    up = lax.ppermute(up, "z", [(z, z + 1) for z in range(step, last)])
+    down = lax.ppermute(down, "z", [(z, z - 1) for z in range(1, Z_CHIPS - step)])
+    return up, down
+
+
+def by_block(z, steps, column):
+    up, down = zip(*steps)
+    if column == 1:
+        return jnp.where(z == 0, down[0], up[0])
+    if column == 2:
+        return jnp.where(z == 0, down[1], jnp.where(z == 3, up[1], down[0]))
+    return jnp.where(
+        z == 0, down[2], jnp.where(z == 1, down[1], jnp.where(z == 2, up[1], up[2]))
+    )
+
+
+def block_table():
+    return jnp.array([[0, 1, 2, 3], [1, 0, 2, 3], [2, 1, 3, 0], [3, 2, 1, 0]], jnp.int32)
+
+
 def by_heads(hidden_in, ln_gain, ln_bias, w_qkv, w_out, cache_kv, cache_len, owner):
     zs, seq_count = lax.axis_size("z"), lax.axis_size("z") * REQ * CORES
     groups = zs * CORES
-    chip = lax.axis_index("r")
+    z, chip, core = lax.axis_index("z"), lax.axis_index("r"), lax.axis_index("c")
     seq = ("z", "r", "c")
     new_dev, depth = hidden_in.shape[1], hidden_in.shape[2]
     width = w_qkv.shape[2]
     cols = width // groups
-
-    w_cut = w_qkv.reshape(3, w_qkv.shape[1], groups, cols).transpose(2, 0, 1, 3)
-    w_own = lax.all_to_all(w_cut, ("z", "c"), split_axis=0, concat_axis=0, tiled=True)
-    swap_x = [(0, 1), (1, 0), (2, 3), (3, 2)]
-    swap_y = [(0, 2), (2, 0), (1, 3), (3, 1)]
-    w_x = lax.ppermute(w_own, "r", swap_x)
-    w_y = lax.ppermute(w_own, "r", swap_y)
-    half = groups // 2
-    w_d = jnp.concatenate(
-        [lax.ppermute(w_x[:half], "r", swap_y), lax.ppermute(w_y[half:], "r", swap_x)], axis=0
-    )
+    blocks = block_table()[z]
+
+    def near(part):
+        return part + (swap_chips(part[0], 1), swap_chips(part[0], 2))
+
+    def far(part):
+        half = part[1].shape[0] // 2
+        return part + (swap_chips(part[1][:half], 2), swap_chips(part[2][half:], 1))
+
+    rows_dev = w_qkv.shape[1]
+    w_cut = w_qkv.reshape(3, rows_dev, groups, cols).transpose(2, 0, 1, 3)
+    slots_here = slots_of(owner[:, 0], seq_count).astype(jnp.bfloat16)
+    slot_rows = jnp.zeros((groups, 8, cols), jnp.bfloat16)
+    slot_rows = slot_rows.at[:, 0, : slots_here.shape[0]].set(slots_here[None])
+    w_cut = jnp.concatenate([w_cut.reshape(groups, 3 * rows_dev, cols), slot_rows], axis=1)
+    w_cut = lax.all_to_all(w_cut, ("z", "c"), split_axis=0, concat_axis=0, tiled=True)
 
     normed = layer_norm(hidden_in, ln_gain, ln_bias)
-    x_own = lax.all_to_all(normed, "r", split_axis=0, concat_axis=0, tiled=True)
-    x_all = lax.all_gather(x_own, ("z", "c"), axis=0, tiled=False)
-
+    x_own = jnp.stack(
+        [
+            swap_chips(lax.dynamic_index_in_dim(normed, chip ^ away, 0, keepdims=False), away)
+            if away
+            else lax.dynamic_index_in_dim(normed, chip, 0, keepdims=False)
+            for away in range(REQ)
+        ]
+    )
     cache_each = cache_kv.shape[1]
     cut = cache_kv.reshape(REQ, cache_each, 2, zs, CORES, cols).transpose(3, 0, 4, 2, 1, 5)
-    cached = lax.all_to_all(
-        cut.reshape(seq_count, 2, cache_each, cols), seq, split_axis=0, concat_axis=0, tiled=True
-    )
-
-    w_out_all = lax.all_gather(w_out, seq, axis=1, tiled=True)
+    cut = cut.reshape(seq_count, 2, cache_each, cols)
 
     length = jnp.sum(jnp.where(jnp.arange(REQ) == chip, cache_len, 0))
     new_len = seq_count * new_dev
     cosine, sine = rotary_tables(length + jnp.arange(new_len))
     shape = (zs, REQ, CORES, new_dev, LANES)
-    query, keys, values, fresh = project(
-        x_all.reshape(groups, REQ, new_dev, depth),
-        (w_own, w_x, w_y, w_d),
-        cosine.reshape(shape),
-        sine.reshape(shape),
-        chip,
-    )
+    tables = [table.reshape(shape).transpose(0, 2, 1, 3, 4) for table in (cosine, sine)]
+
+    x_own, w_cut = lax.optimization_barrier((x_own, w_cut))
+    w_own = w_cut[:, : 3 * rows_dev].reshape(groups, 3, rows_dev, cols)
+    slot_ids = w_cut[:, 3 * rows_dev, : slots_here.shape[0]].astype(jnp.int32)
+    slot_ids = slot_ids.reshape(zs, CORES, REQ, new_dev)[blocks]
+    slot_ids = slot_ids[:, :, chip ^ jnp.arange(REQ)].reshape(zs, CORES, 1, REQ * new_dev)
+
+    out_parts = [lax.all_gather(w_out, "r", axis=0, tiled=False)]
+
+    w_parts = [(w_own[:, :2],), (w_own[:, 2:],)]
+    x_steps = [z_step(x_own, x_own, 0)]
+    other_own = swap_cores(x_own)
+    w_parts = [near(w_parts[0]), w_parts[1]]
+    x_steps, w_parts, other_own, tables, out_parts = lax.optimization_barrier(
+        (x_steps, w_parts, other_own, tables, out_parts)
+    )
+    x_steps = x_steps + [z_step(*x_steps[0], 1)]
+    x_first = by_block(z, x_steps, 1)
+    other_first = swap_cores(x_first)
+    w_parts = [far(w_parts[0]), near(w_parts[1])]
+    x_steps, w_parts, x_first, other_first = lax.optimization_barrier(
+        (x_steps, w_parts, x_first, other_first)
+    )
+    x_steps = x_steps + [z_step(*x_steps[1], 2)]
+    x_second = by_block(z, x_steps, 2)
+    other_second = swap_cores(x_second)
+    w_parts = [w_parts[0], far(w_parts[1])]
+    weights = [piece for part in w_parts for piece in part]
+
+    def run(first, pairs, held, cost):
+        steps = len(pairs) // CORES
+        place = jnp.concatenate([jnp.stack([chip, core]), blocks[first : first + steps]])
+        *held, fresh = project(pairs, weights, *tables, place.astype(jnp.int32), held, cost)
+        return held, fresh
+
+    def send(fresh):
+        return [fresh[0]] + [swap_chips(fresh[away], away) for away in range(1, REQ)]
+
+    held, fresh = run(0, [x_own, other_own, x_first, other_first], (), 0)
+    x_steps, held, fresh, x_second, other_second, w_out = lax.optimization_barrier(
+        (x_steps, held, fresh, x_second, other_second, w_out)
+    )
+    out_steps = [z_step(w_out, w_out, 0)]
+    x_last = by_block(z, x_steps, 3)
+    sent = send(fresh)
+    cached = lax.all_to_all(cut, seq, split_axis=0, concat_axis=0, tiled=True)
+    held, fresh = run(2, [x_second, other_second, x_last, swap_cores(x_last)], held, 1)
+    out_steps, sent, held, fresh, cached = lax.optimization_barrier(
+        (out_steps, sent, held, fresh, cached)
+    )
+    w_first = by_block(z, out_steps, 1)
+    w_first = far(near((w_first.reshape(2, w_first.shape[0] // 2, w_first.shape[1]),)))
+    out_steps += [z_step(*out_steps[0], 1)]
+    out_steps += [z_step(*out_steps[1], 2)]
+    sent += send(fresh)
+    query, keys, values = held
     flat = (new_len, cols)
-
-    whole = lax.all_to_all(fresh, "r", split_axis=0, concat_axis=0, tiled=True)
-    slot_ids = lax.all_gather(slots_of(owner[:, 0], seq_count), ("z", "c"), axis=0, tiled=False)
-    slot_ids = slot_ids.reshape(groups, REQ * new_dev)
 
     attended = attend(
         query.reshape(flat), keys.reshape(flat), values.reshape(flat), cached, length
     )
+    out_steps, attended, sent, w_first = lax.optimization_barrier(
+        (out_steps, attended, sent, w_first)
+    )
+    out_parts += w_first
+    rest = near((jnp.stack([by_block(z, out_steps, 2), by_block(z, out_steps, 3)]),))
     back = lax.all_to_all(
         attended.reshape(seq_count, new_dev, cols), seq, split_axis=0, concat_axis=0, tiled=True
     )
-
-    rows = whole.reshape(REQ, groups, new_dev, 2 * cols).transpose(1, 0, 2, 3)
-    rows = rows.reshape(groups, REQ * new_dev, 2 * cols)
-    placing = (
-        jnp.arange(seq_count * SLOTS)[None, :, None] == slot_ids[:, None, :]
-    ).astype(jnp.bfloat16)
-    outgoing = jnp.einsum("gst,gtw->gsw", placing, rows, preferred_element_type=jnp.float32)
-    outgoing = outgoing.astype(jnp.bfloat16).reshape(groups, seq_count, SLOTS, 2 * cols)
-    arrived = lax.all_to_all(
-        outgoing.transpose(1, 0, 2, 3), seq, split_axis=0, concat_axis=0, tiled=True
-    )
+    outgoing = order(blocks, slot_ids, sent, seq_count)
+    back, outgoing, rest = lax.optimization_barrier((back, outgoing, rest))
+    out_parts += far(rest)
+    arrived = lax.all_to_all(outgoing, seq, split_axis=0, concat_axis=0, tiled=True)
     appended = arrived.reshape(zs, REQ, CORES, zs, CORES, SLOTS, 2, cols)
     appended = appended.transpose(3, 1, 4, 5, 6, 0, 2, 7).reshape(seq_count * SLOTS, 2, width)
 
-    rows_back = back.reshape(zs, REQ, CORES, new_dev, cols).transpose(1, 3, 0, 2, 4)
-    out = jnp.dot(
-        rows_back.reshape(REQ * new_dev, width), w_out_all, preferred_element_type=jnp.float32
-    ).astype(jnp.bfloat16)
+    place = jnp.concatenate([jnp.stack([chip]), blocks]).astype(jnp.int32)
+    out, out_other = output(place, back, swap_cores(back), out_parts)
+    out = interleave(core, out, swap_cores(out_other))
     return out.reshape(REQ, new_dev, out.shape[1]), appended
 
 
@@ -435,6 +731,7 @@
         heads_here = args[3].shape[2] // tp_count // HD
         split = (
             tp_count == 1
+            and zs == Z_CHIPS
             and zs * REQ * CORES == seq_count
             and heads_here % max(zs * CORES, 1) == 0
         )

time: 728 us -> 609 us (0.84)
  blocking collectives: 253 us -> 0 us
  waiting for transfers between devices: 188 us -> 316 us
  starting transfers between devices: 133 us -> 89.1 us
  Pallas kernels: 61.6 us -> 97.7 us
  matrix products: 17.9 us -> 0 us
  other arithmetic: 15.3 us -> 28.1 us
  local copies, waits for them, and re-layouts: 40 us -> 52 us
    ppermute x4 -> x43, waiting for transfers between devices: 84.1 us -> 288 us  [the longest x25 260 us: swap_chips(): lax.ppermute(value, 'r', [(chip, chip ^ away) for chip in range(REQ)])]
    all_to_all x2 -> x0, blocking collectives: 185 us -> none  [the longest x1 158 us: by_heads(): lax.all_to_all(w_cut, ('z', 'c'), split_axis=0, concat_axis=0, tiled=True)]
    all_to_all x3, waiting for transfers between devices: 103 us -> 27.3 us  [the longest x1 27.3 us: by_heads(): lax.all_to_all(w_cut, ('z', 'c'), split_axis=0, concat_axis=0, tiled=True)]
    all_gather x1 -> x0, blocking collectives: 67.8 us -> none  [by_heads(): lax.all_gather(slots_of(owner[:, 0], seq_count), ('z', 'c'), axis=0, tile...]
    all_to_all x1, starting transfers between devices: 62.3 us -> 6.12 us  [by_heads(): lax.all_to_all(attended.reshape(seq_count, new_dev, cols), seq, split_axi...]
    ppermute x4 -> x43, starting transfers between devices: 10.8 us -> 63.1 us  [the longest x25 24.4 us: swap_chips(): lax.ppermute(value, 'r', [(chip, chip ^ away) for chip in range(REQ)])]
    all_to_all x3, starting transfers between devices: 59.6 us -> 19.9 us  [the longest x1 8.77 us: by_heads(): cached = lax.all_to_all(cut, seq, split_axis=0, concat_axis=0, tiled=True)]
    pallas_call x0 -> x3, Pallas kernels: none -> 27.3 us  [the longest x1 18.5 us: output(): pl.pallas_call(output_kernel, grid_spec=pltpu.PrefetchScalarGridSpec(num_...]
  transfers between devices with their start and end apart: 10 -> 48, of which waited for: 5 -> 25; matrix products, arithmetic and copies ran while one was open for 7% -> 6% of each run, Pallas kernels for 9% -> 16%
where the time goes in v2:
time: 609 us; the launch traced here: 598 us
  waiting for transfers between devices  316 us (52%)
  Pallas kernels  97.7 us (16%)
  starting transfers between devices  89.1 us (15%)
  local copies, waits for them, and re-layouts  52 us (9%)
  other arithmetic  28.1 us (5%)
  between operations  15.1 us (2%)
    ppermute x25, waiting for transfers between devices, swap_chips(): lax.ppermute(value, 'r', [(chip, chip ^ away) for chip in range(REQ)])  260 us
    pallas_call x2, Pallas kernels, project(): pl.pallas_call(project_kernel, grid_spec=pltpu.PrefetchScalarGridSpec(num...  45.1 us
    all_to_all x1, waiting for transfers between devices, by_heads(): lax.all_to_all(w_cut, ('z', 'c'), split_axis=0, concat_axis=0, tiled=True)  27.3 us
    pallas_call x1, Pallas kernels, attend(): pl.pallas_call(functools.partial(attend_kernel, blocks=blocks), grid_spec...  25.2 us
    ppermute x25, starting transfers between devices, swap_chips(): lax.ppermute(value, 'r', [(chip, chip ^ away) for chip in range(REQ)])  24.4 us
    pallas_call x1, Pallas kernels, output(): pl.pallas_call(output_kernel, grid_spec=pltpu.PrefetchScalarGridSpec(num_...  18.5 us
    ppermute x6, starting transfers between devices, z_step(): up = lax.ppermute(up, 'z', [(z, z + 1) for z in range(step, last)])  16.2 us
    ppermute x6, starting transfers between devices, z_step(): lax.ppermute(down, 'z', [(z, z - 1) for z in range(1, Z_CHIPS - step)])  15.9 us
  transfers between devices with their start and end apart: 48, of which 25 were waited for; matrix products, arithmetic and copies ran while one was open for 6% of the time, Pallas kernels for 16%

profile of v2, /device:TPU:17, one launch (start us, length us, event | category | flops | bytes accessed | tf_op | source)
XLA Modules:
  0.0 598.0 jit_solution(17192924826484613542)
XLA Ops:
  16.7 5.7 all-to-all-start
  28.1 14.5 %collective-permute-done.2 = bf16[64,4096]{1,0:T(8,128)(2,1)S(1)} collective-permute-done((bf16[64,4096]{1,0:T(8,128)(2,1)S(1)}, bf16[64,4096]{1,0:T(8,128)(2,1)S(1)}, u32[]{:S(2)}, u32[]{:S(2)}) %collective-permute-start.2) | collective-permute-done | bytes 524320 | tf_op jit(solution)/shard_map/ppermute | solution.py:472
  42.6 20.0 %collective-permute-done.1 = bf16[64,4096]{1,0:T(8,128)(2,1)S(1)} collective-permute-done((bf16[64,4096]{1,0:T(8,128)(2,1)S(1)}, bf16[64,4096]{1,0:T(8,128)(2,1)S(1)}, u32[]{:S(2)}, u32[]{:S(2)}) %collective-permute-start.1) | collective-permute-done | bytes 524320 | tf_op jit(solution)/shard_map/ppermute | solution.py:472
  64.2 27.3 %all-to-all-done = bf16[8,392,512]{2,1,0:T(8,128)(2,1)} async-done(((bf16[8,392,512]{2,1,0:T(8,128)(2,1)}), bf16[8,392,512]{2,1,0:T(8,128)(2,1)}, u32[]{:S(2)}, u32[]{:S(2)}) %all-to-all-start) | async-done | bytes 3211296 | tf_op jit(solution)/shard_map/all_to_all | solution.py:524
  107.0 5.6 fusion.8
  113.8 28.1 %collective-permute-done.6.refs_2_ = bf16[8,2,128,512]{3,2,1,0:T(8,128)(2,1)} collective-permute-done((bf16[8,2,128,512]{3,2,1,0:T(8,128)(2,1)}, bf16[8,2,128,512]{3,2,1,0:T(8,128)(2,1)}, u32[]{:S(2)}, u32[]{:S(2)}) %collective-permute-start.6) | collective-permute-done | bytes 2097184 | tf_op jit(solution)/shard_map/ppermute | solution.py:472
  142.8 5.8 collective-permute-done.4
  166.9 12.3 %collective-permute-done.11.refs_4_ = bf16[4,2,128,512]{3,2,1,0:T(8,128)(2,1)S(1)} collective-permute-done((bf16[4,2,128,512]{3,2,1,0:T(8,128)(2,1)S(1)}, bf16[4,2,128,512]{3,2,1,0:T(8,128)(2,1)S(1)}, u32[]{:S(2)}, u32[]{:S(2)}) %collective-permute-start.11) | collective-permute-done | bytes 1048608 | tf_op jit(solution)/shard_map/ppermute | solution.py:472
  181.5 20.9 %collective-permute-done.13.refs_7_ = bf16[8,1,128,512]{3,2,1,0:T(8,128)(2,1)} collective-permute-done((bf16[8,1,128,512]{3,2,1,0:T(8,128)(2,1)S(1)}, bf16[8,1,128,512]{3,2,1,0:T(8,128)(2,1)}, u32[]{:S(2)}, u32[]{:S(2)}) %collective-permute-start.13) | collective-permute-done | bytes 1048608 | tf_op jit(solution)/shard_map/ppermute | solution.py:472
  225.8 10.1 %collective-permute-done.18.refs_9_ = bf16[4,1,128,512]{3,2,1,0:T(8,128)(2,1)S(1)} collective-permute-done((bf16[4,1,128,512]{3,2,1,0:T(8,128)(2,1)}, bf16[4,1,128,512]{3,2,1,0:T(8,128)(2,1)S(1)}, u32[]{:S(2)}, u32[]{:S(2)}) %collective-permute-start.18) | collective-permute-done | bytes 524320 | tf_op jit(solution)/shard_map/ppermute | solution.py:472
  237.6 22.6 %shard_map.104 = (bf16[4,4,2,64,512]{4,3,2,1,0:T(8,128)(2,1)}, bf16[4,4,2,64,512]{4,3,2,1,0:T(8,128)(2,1)}, bf16[4,4,2,64,512]{4,3,2,1,0:T(8,128)(2,1)}, bf16[4,2,2,64,1024]{4,3,2,1,0:T(8,128)(2,1)}) custom-call(s32[4]{0:T(128)} %pad_add_fusion.1.place, bf16[8,2,128,512]{3,2,1,0:T(8,128)(2,1)} %slice.132.refs_0_, ...), custom_call_target="tpu_custom_call" | custom-call | tf_op jit(solution)/shard_map/pallas_call | solution.py:158
  268.1 8.8 %all-to-all-start.1 = ((bf16[32,2,16,512]{3,2,1,0:T(8,128)(2,1)}), bf16[32,2,16,512]{3,2,1,0:T(8,128)(2,1)S(1)}, u32[]{:S(2)}, u32[]{:S(2)}) async-start(bf16[32,2,16,512]{3,2,1,0:T(8,128)(2,1)} %bitcast.25), calls=%async_computation.1 | async-start | bytes 2097152 | tf_op jit(solution)/shard_map/all_to_all | solution.py:589
  288.4 22.5 %shard_map.105 = (bf16[4,4,2,64,512]{4,3,2,1,0:T(8,128)(2,1)}, bf16[4,4,2,64,512]{4,3,2,1,0:T(8,128)(2,1)}, bf16[4,4,2,64,512]{4,3,2,1,0:T(8,128)(2,1)}, bf16[4,2,2,64,1024]{4,3,2,1,0:T(8,128)(2,1)}) custom-call(s32[4]{0:T(128)} %pad_add_fusion.3.place, ...), custom_call_target="tpu_custom_call", output_to_operand_aliasing={{0}: (17, {}), {1}: (18, {}), {2}: (19, {})} | custom-call | flops 12884901888 | bytes 20971520 | tf_op jit(solution)/shard_map/pallas_call | solution.py:158
  310.9 5.6 collective-permute-done.23.refs_2_
  333.8 15.0 %collective-permute-done.34.refs_5_ = bf16[2,2048,128]{2,1,0:T(8,128)(2,1)S(1)} collective-permute-done((bf16[2,2048,128]{2,1,0:T(8,128)(2,1)S(1)}, bf16[2,2048,128]{2,1,0:T(8,128)(2,1)S(1)}, u32[]{:S(2)}, u32[]{:S(2)}) %collective-permute-start.34) | collective-permute-done | bytes 1048608 | tf_op jit(solution)/shard_map/ppermute | solution.py:472
  356.9 9.1 %collective-permute-done.32.refs_7_ = bf16[2,2,64,1024]{3,2,1,0:T(8,128)(2,1)} collective-permute-done((bf16[2,2,64,1024]{3,2,1,0:T(8,128)(2,1)S(1)}, bf16[2,2,64,1024]{3,2,1,0:T(8,128)(2,1)}, u32[]{:S(2)}, u32[]{:S(2)}) %collective-permute-start.32) | collective-permute-done | bytes 524320 | tf_op jit(solution)/shard_map/ppermute | solution.py:472
  373.9 25.2 %shard_map.106 = bf16[2048,512]{1,0:T(8,128)(2,1)} custom-call(s32[1]{0:T(128)} %bitcast.26.length, bf16[2048,512]{1,0:T(8,128)(2,1)S(1)} %bitcast.94, bf16[2048,512]{1,0:T(8,128)(2,1)} %bitcast.112, bf16[2048,512]{1,0:T(8,128)(2,1)} %bitcast.113, bf16[32,2,16,512]{3,2,1,0:T(8,128)(2,1)S(1)} %all-to-all-done.1.kc_ref.vc_ref, ...), custom_call_target="tpu_custom_call" | custom-call | flops 6442450944 | bytes 8388608 | tf_op jit(solution)/shard_map/pallas_call | solution.py:304
  400.9 6.1 %all-to-all-start.2 = ((bf16[32,64,512]{2,1,0:T(8,128)(2,1)}), bf16[32,64,512]{2,1,0:T(8,128)(2,1)}, u32[]{:S(2)}, u32[]{:S(2)}) async-start(bf16[32,64,512]{2,1,0:T(8,128)(2,1)} %bitcast.35), calls=%async_computation.2 | async-start | bytes 4194304 | tf_op jit(solution)/shard_map/all_to_all | solution.py:610
  412.8 6.1 %shard_map.107 = bf16[32,4,16,1024]{3,2,1,0:T(8,128)(2,1)} custom-call(s32[4]{0:T(128)} %get-tuple-element.193.blocks, s32[4,2,1,256]{3,2,1,0:T(1,128)} %reshape.276.slot_ref, bf16[2,2,64,1024]{3,2,1,0:T(8,128)(2,1)} %get-tuple-element.150.refs_0_, bf16[2,2,64,1024]{3,2,1,0:T(8,128)(2,1)} %collective-permute-done.22.refs_1_, ...), custom_call_target="tpu_custom_call" | custom-call | flops 1073741824 | bytes 8388608 | tf_op jit(solution)/shard_map/pallas_call | solution.py:223
  418.9 58.1 %collective-permute-done.38.refs_10_ = bf16[2,4096,128]{2,1,0:T(8,128)(2,1)} collective-permute-done((bf16[2,4096,128]{2,1,0:T(8,128)(2,1)S(1)}, bf16[2,4096,128]{2,1,0:T(8,128)(2,1)}, u32[]{:S(2)}, u32[]{:S(2)}) %collective-permute-start.38) | collective-permute-done | bytes 2097184 | tf_op jit(solution)/shard_map/ppermute | solution.py:472
  488.5 57.0 %collective-permute-done.41.refs_12_ = bf16[1,4096,128]{2,1,0:T(8,128)(2,1)S(1)} collective-permute-done((bf16[1,4096,128]{2,1,0:T(8,128)(2,1)S(1)}, bf16[1,4096,128]{2,1,0:T(8,128)(2,1)S(1)}, u32[]{:S(2)}, u32[]{:S(2)}) %collective-permute-start.41) | collective-permute-done | bytes 1048608 | tf_op jit(solution)/shard_map/ppermute | solution.py:472
  548.2 18.5 %shard_map.108 = (bf16[256,2048]{1,0:T(8,128)(2,1)}, bf16[256,2048]{1,0:T(8,128)(2,1)}) custom-call(s32[5]{0:T(128)} %pad_add_fusion.place, bf16[32,64,512]{2,1,0:T(8,128)(2,1)} %all-to-all-done.2.refs_0_, bf16[32,64,512]{2,1,0:T(8,128)(2,1)} %copy-done.27, bf16[4,4096,128]{2,1,0:T(8,128)(2,1)} %bitcast.111, bf16[2,2048,128]{2,1,0:T(8,128)(2,1)} %bitcast.103, ...), custom_call_target="tpu_custom_call" | custom-call | flops 8589934592 | bytes 20971520 | tf_op jit(solution)/shard_map/pallas_call | solution.py:409
  574.5 8.6 %copy.27 = bf16[4,4,2,8,2,4,2,512]{7,6,5,4,3,2,1,0:T(2,128)(2,1)} copy(bf16[4,4,2,8,2,4,2,512]{7,3,4,2,0,6,1,5:T(8,128)(2,1)} %bitcast.44) | data formatting | bytes 8388608 | tf_op jit(solution)/shard_map/transpose | solution.py:618
  583.1 7.6 %reshape.279 = bf16[256,2,4096]{2,1,0:T(2,128)(2,1)} reshape(bf16[4,4,2,8,2,4,2,512]{7,6,5,4,3,2,1,0:T(2,128)(2,1)} %copy.27) | data formatting | bytes 8388608 | tf_op jit(solution)/shard_map/reshape | solution.py:618
  (209 shorter events, 161.9 us)
Async XLA Ops:
  16.7 74.8 %all-to-all-start = ((bf16[8,392,512]{2,1,0:T(8,128)(2,1)}), bf16[8,392,512]{2,1,0:T(8,128)(2,1)}, u32[]{:S(2)}, u32[]{:S(2)}) async-start(bf16[8,392,512]{2,1,0:T(8,128)(2,1)} %pad_maximum_fusion), calls=%async_computation | async-start | bytes 6422528 | tf_op jit(solution)/shard_map/all_to_all | solution.py:524
  22.3 91.5 %all-gather.3.cloned.1.call-start = ((), (), s32[]{:S(2)}) async-start(), calls=%async_computation.4 | async-start | bytes 5242880 | tf_op jit(solution)/shard_map/all_gather | solution.py:551
  95.2 46.6 %collective-permute-start.6 = (bf16[8,2,128,512]{3,2,1,0:T(8,128)(2,1)}, bf16[8,2,128,512]{3,2,1,0:T(8,128)(2,1)}, u32[]{:S(2)}, u32[]{:S(2)}) collective-permute-start(bf16[8,2,128,512]{3,2,1,0:T(8,128)(2,1)} %slice.132.refs_0_), channel_id=1, source_target_pairs={{0,4},{2,6},{4,0},{6,2},{1,5},{3,7},{5,1},{7,3},{8,12},{10,14},{12... | collective-permute-start | bytes 6291464 | tf_op jit(solution)/shard_map/ppermute | solution.py:472
  96.5 46.3 %collective-permute-start.5 = (bf16[8,2,128,512]{3,2,1,0:T(8,128)(2,1)}, bf16[8,2,128,512]{3,2,1,0:T(8,128)(2,1)}, u32[]{:S(2)}, u32[]{:S(2)}) collective-permute-start(bf16[8,2,128,512]{3,2,1,0:T(8,128)(2,1)} %slice.132.refs_0_), channel_id=1, source_target_pairs={{0,2},{2,0},{4,6},{6,4},{1,3},{3,1},{5,7},{7,5},{8,10},{10,8},{12,... | collective-permute-start | bytes 6291464 | tf_op jit(solution)/shard_map/ppermute | solution.py:472
  97.7 45.1 %collective-permute-start.7 = (bf16[4,64,4096]{2,1,0:T(8,128)(2,1)}, bf16[4,64,4096]{2,1,0:T(8,128)(2,1)}, u32[]{:S(2)}, u32[]{:S(2)}) collective-permute-start(bf16[4,64,4096]{2,1,0:T(8,128)(2,1)} %pad_maximum_fusion.1.refs_12_), channel_id=1, source_target_pairs={{0,1},{1,0},{2,3},{3,2},{4,5},{5,4},{6,7},{7,6},{8,9},{9,8},{10,11... | collective-permute-start | bytes 6291464 | tf_op jit(solution)/shard_map/ppermute | solution.py:476
  99.1 49.5 %collective-permute-start.4 = (bf16[4,64,4096]{2,1,0:T(8,128)(2,1)}, bf16[4,64,4096]{2,1,0:T(8,128)(2,1)}, u32[]{:S(2)}, u32[]{:S(2)}) collective-permute-start(bf16[4,64,4096]{2,1,0:T(8,128)(2,1)} %pad_maximum_fusion.1.refs_12_), channel_id=1, source_target_pairs={{8,0},{16,8},{24,16},{9,1},{17,9},{25,17},{10,2},{18,10},{26,18},{... | collective-permute-start | bytes 6291464 | tf_op jit(solution)/shard_map/ppermute | solution.py:482
  101.1 51.3 %collective-permute-start.3 = (bf16[4,64,4096]{2,1,0:T(8,128)(2,1)}, bf16[4,64,4096]{2,1,0:T(8,128)(2,1)}, u32[]{:S(2)}, u32[]{:S(2)}) collective-permute-start(bf16[4,64,4096]{2,1,0:T(8,128)(2,1)} %pad_maximum_fusion.1.refs_12_), channel_id=1, source_target_pairs={{0,8},{8,16},{16,24},{1,9},{9,17},{17,25},{2,10},{10,18},{18,26},{... | collective-permute-start | bytes 6291464 | tf_op jit(solution)/shard_map/ppermute | solution.py:481
  157.5 46.9 %collective-permute-start.14 = (bf16[4,64,4096]{2,1,0:T(8,128)(2,1)S(1)}, bf16[4,64,4096]{2,1,0:T(8,128)(2,1)}, u32[]{:S(2)}, u32[]{:S(2)}) collective-permute-start(bf16[4,64,4096]{2,1,0:T(8,128)(2,1)S(1)} %broadcast_select_fusion.refs_14_), channel_id=1, source_target_pairs={{0,1},{1,0},{2,3},{3,2},{4,5},{5,4},{6,7},{7,6},{8,9},{9,8},{10,11... | collective-permute-start | bytes 6291464 | tf_op jit(solution)/shard_map/ppermute | solution.py:476
  158.9 49.4 %collective-permute-start.8 = (bf16[4,64,4096]{2,1,0:T(8,128)(2,1)}, bf16[4,64,4096]{2,1,0:T(8,128)(2,1)}, u32[]{:S(2)}, u32[]{:S(2)}) collective-permute-start(bf16[4,64,4096]{2,1,0:T(8,128)(2,1)} %collective-permute-done.3), channel_id=1, source_target_pairs={{8,16},{16,24},{9,17},{17,25},{10,18},{18,26},{11,19},{19,27},{12,... | collective-permute-start | bytes 6291464 | tf_op jit(solution)/shard_map/ppermute | solution.py:481
  161.6 48.9 %collective-permute-start.9 = (bf16[4,64,4096]{2,1,0:T(8,128)(2,1)}, bf16[4,64,4096]{2,1,0:T(8,128)(2,1)}, u32[]{:S(2)}, u32[]{:S(2)}) collective-permute-start(bf16[4,64,4096]{2,1,0:T(8,128)(2,1)} %collective-permute-done.4), channel_id=1, source_target_pairs={{8,0},{16,8},{9,1},{17,9},{10,2},{18,10},{11,3},{19,11},{12,4},{20... | collective-permute-start | bytes 6291464 | tf_op jit(solution)/shard_map/ppermute | solution.py:482
  213.7 46.5 %collective-permute-start.19 = (bf16[4,64,4096]{2,1,0:T(8,128)(2,1)}, bf16[4,64,4096]{2,1,0:T(8,128)(2,1)}, u32[]{:S(2)}, u32[]{:S(2)}) collective-permute-start(bf16[4,64,4096]{2,1,0:T(8,128)(2,1)} %select_select_fusion.1.refs_12_), channel_id=1, source_target_pairs={{0,1},{1,0},{2,3},{3,2},{4,5},{5,4},{6,7},{7,6},{8,9},{9,8},{10,11... | collective-permute-start | bytes 6291464 | tf_op jit(solution)/shard_map/ppermute | solution.py:476
  214.8 46.8 %collective-permute-start.15 = (bf16[4,64,4096]{2,1,0:T(8,128)(2,1)}, bf16[4,64,4096]{2,1,0:T(8,128)(2,1)S(1)}, u32[]{:S(2)}, u32[]{:S(2)}) collective-permute-start(bf16[4,64,4096]{2,1,0:T(8,128)(2,1)} %collective-permute-done.8), channel_id=1, source_target_pairs={{16,24},{17,25},{18,26},{19,27},{20,28},{21,29},{22,30},{23,31}} | collective-permute-start | bytes 6291464 | tf_op jit(solution)/shard_map/ppermute | solution.py:481
  216.2 45.4 %collective-permute-start.16 = (bf16[4,64,4096]{2,1,0:T(8,128)(2,1)}, bf16[4,64,4096]{2,1,0:T(8,128)(2,1)}, u32[]{:S(2)}, u32[]{:S(2)}) collective-permute-start(bf16[4,64,4096]{2,1,0:T(8,128)(2,1)} %collective-permute-done.9), channel_id=1, source_target_pairs={{8,0},{9,1},{10,2},{11,3},{12,4},{13,5},{14,6},{15,7}} | collective-permute-start | bytes 6291464 | tf_op jit(solution)/shard_map/ppermute | solution.py:482
  277.5 44.4 %collective-permute-start.21 = (bf16[4096,128]{1,0:T(8,128)(2,1)S(1)}, bf16[4096,128]{1,0:T(8,128)(2,1)S(1)}, u32[]{:S(2)}, u32[]{:S(2)}) collective-permute-start(bf16[4096,128]{1,0:T(8,128)(2,1)S(1)} %copy-done.10), channel_id=1, source_target_pairs={{8,0},{16,8},{24,16},{9,1},{17,9},{25,17},{10,2},{18,10},{26,18},{... | collective-permute-start | bytes 3145736 | tf_op jit(solution)/shard_map/ppermute | solution.py:482
  279.7 43.5 %collective-permute-start.20 = (bf16[4096,128]{1,0:T(8,128)(2,1)S(1)}, bf16[4096,128]{1,0:T(8,128)(2,1)}, u32[]{:S(2)}, u32[]{:S(2)}) collective-permute-start(bf16[4096,128]{1,0:T(8,128)(2,1)S(1)} %copy-done.10), channel_id=1, source_target_pairs={{0,8},{8,16},{16,24},{1,9},{9,17},{17,25},{2,10},{10,18},{18,26},{... | collective-permute-start | bytes 3145736 | tf_op jit(solution)/shard_map/ppermute | solution.py:481
  352.2 47.0 %collective-permute-start.28 = (bf16[4096,128]{1,0:T(8,128)(2,1)S(1)}, bf16[4096,128]{1,0:T(8,128)(2,1)S(1)}, u32[]{:S(2)}, u32[]{:S(2)}) collective-permute-start(bf16[4096,128]{1,0:T(8,128)(2,1)S(1)} %collective-permute-done.26), channel_id=1, source_target_pairs={{16,24},{17,25},{18,26},{19,27},{20,28},{21,29},{22,30},{23,31}} | collective-permute-start | bytes 3145736 | tf_op jit(solution)/shard_map/ppermute | solution.py:481
  354.6 44.6 %collective-permute-start.29 = (bf16[4096,128]{1,0:T(8,128)(2,1)S(1)}, bf16[4096,128]{1,0:T(8,128)(2,1)S(1)}, u32[]{:S(2)}, u32[]{:S(2)}) collective-permute-start(bf16[4096,128]{1,0:T(8,128)(2,1)S(1)} %collective-permute-done.27), channel_id=1, source_target_pairs={{8,0},{9,1},{10,2},{11,3},{12,4},{13,5},{14,6},{15,7}} | collective-permute-start | bytes 3145736 | tf_op jit(solution)/shard_map/ppermute | solution.py:482
  400.9 76.1 %all-to-all-start.2 = ((bf16[32,64,512]{2,1,0:T(8,128)(2,1)}), bf16[32,64,512]{2,1,0:T(8,128)(2,1)}, u32[]{:S(2)}, u32[]{:S(2)}) async-start(bf16[32,64,512]{2,1,0:T(8,128)(2,1)} %bitcast.35), calls=%async_computation.2 | async-start | bytes 4194304 | tf_op jit(solution)/shard_map/all_to_all | solution.py:610
  407.6 69.4 %collective-permute-start.38 = (bf16[2,4096,128]{2,1,0:T(8,128)(2,1)S(1)}, bf16[2,4096,128]{2,1,0:T(8,128)(2,1)}, u32[]{:S(2)}, u32[]{:S(2)}) collective-permute-start(bf16[2,4096,128]{2,1,0:T(8,128)(2,1)S(1)} %pad_maximum_fusion.2.refs_8_), channel_id=1, source_target_pairs={{0,4},{2,6},{4,0},{6,2},{1,5},{3,7},{5,1},{7,3},{8,12},{10,14},{12... | collective-permute-start | bytes 6291464 | tf_op jit(solution)/shard_map/ppermute | solution.py:472
  408.8 68.2 %collective-permute-start.37 = (bf16[2,4096,128]{2,1,0:T(8,128)(2,1)S(1)}, bf16[2,4096,128]{2,1,0:T(8,128)(2,1)}, u32[]{:S(2)}, u32[]{:S(2)}) collective-permute-start(bf16[2,4096,128]{2,1,0:T(8,128)(2,1)S(1)} %pad_maximum_fusion.2.refs_8_), channel_id=1, source_target_pairs={{0,2},{2,0},{4,6},{6,4},{1,3},{3,1},{5,7},{7,5},{8,10},{10,8},{12,... | collective-permute-start | bytes 6291464 | tf_op jit(solution)/shard_map/ppermute | solution.py:472
  477.0 97.5 %all-to-all-start.3 = ((bf16[32,4,16,1024]{3,2,1,0:T(8,128)(2,1)}), bf16[32,4,16,1024]{3,2,1,0:T(8,128)(2,1)}, u32[]{:S(2)}, u32[]{:S(2)}) async-start(bf16[32,4,16,1024]{3,2,1,0:T(8,128)(2,1)} %shard_map.107), calls=%async_computation.3 | async-start | bytes 8388608 | tf_op jit(solution)/shard_map/all_to_all | solution.py:616
  482.5 63.0 %collective-permute-start.39 = (bf16[32,64,512]{2,1,0:T(8,128)(2,1)}, bf16[32,64,512]{2,1,0:T(8,128)(2,1)S(1)}, u32[]{:S(2)}, u32[]{:S(2)}) collective-permute-start(bf16[32,64,512]{2,1,0:T(8,128)(2,1)} %all-to-all-done.2.refs_0_), channel_id=1, source_target_pairs={{0,1},{1,0},{2,3},{3,2},{4,5},{5,4},{6,7},{7,6},{8,9},{9,8},{10,11... | collective-permute-start | bytes 6291464 | tf_op jit(solution)/shard_map/ppermute | solution.py:476
  485.5 60.0 %collective-permute-start.41 = (bf16[1,4096,128]{2,1,0:T(8,128)(2,1)S(1)}, bf16[1,4096,128]{2,1,0:T(8,128)(2,1)S(1)}, u32[]{:S(2)}, u32[]{:S(2)}) collective-permute-start(bf16[1,4096,128]{2,1,0:T(8,128)(2,1)S(1)} %slice.126), channel_id=1, source_target_pairs={{0,2},{2,0},{4,6},{6,4},{1,3},{3,1},{5,7},{7,5},{8,10},{10,8},{12,... | collective-permute-start | bytes 3145736 | tf_op jit(solution)/shard_map/ppermute | solution.py:472
  486.7 58.8 %collective-permute-start.40 = (bf16[1,4096,128]{2,1,0:T(8,128)(2,1)S(1)}, bf16[1,4096,128]{2,1,0:T(8,128)(2,1)S(1)}, u32[]{:S(2)}, u32[]{:S(2)}) collective-permute-start(bf16[1,4096,128]{2,1,0:T(8,128)(2,1)S(1)} %slice.125), channel_id=1, source_target_pairs={{0,4},{2,6},{4,0},{6,2},{1,5},{3,7},{5,1},{7,3},{8,12},{10,14},{12... | collective-permute-start | bytes 3145736 | tf_op jit(solution)/shard_map/ppermute | solution.py:472
  (57 other events, 1023.5 us)
Sparse Core Ops, SparseCore 0:
  25.0 68.1 all-gather.2

commit v3 on v2

--- a/solution.py
+++ b/solution.py
@@ -57,7 +57,7 @@
     return cosine, sine
 
 
-def project_kernel(place, *refs):
+def project_kernel(place, *refs, by_chip):
     q_ref, k_ref, v_ref, send_ref, rows_ref, held, sem_x, sem_w = refs[-8:]
     steps, _, _, each, depth = rows_ref.shape
     weights, (cos_ref, sin_ref) = refs[:10], refs[10:12]
@@ -140,13 +140,13 @@
                     q_ref[0, r, c] = part
                 elif which == 1:
                     k_ref[0, r, c] = part
-                    send_ref[r ^ chip, 0, c, :, :width] = part
+                    send_ref[r if by_chip else r ^ chip, 0, c, :, :width] = part
                 else:
                     v_ref[0, r, c] = part
-                    send_ref[r ^ chip, 0, c, :, width:] = part
-
-
-def project(x_pairs, weights, cosine, sine, place, held, cost):
+                    send_ref[r if by_chip else r ^ chip, 0, c, :, width:] = part
+
+
+def project(x_pairs, weights, cosine, sine, place, held, cost, by_chip):
     steps = len(x_pairs) // CORES
     _, each, depth = x_pairs[0].shape
     groups, _, rows_each, width = weights[0].shape
@@ -156,7 +156,7 @@
     whole = jax.ShapeDtypeStruct((zs, REQ, CORES, each, width), jnp.bfloat16)
     anywhere = pl.BlockSpec(memory_space=pl.ANY)
     return pl.pallas_call(
-        project_kernel,
+        functools.partial(project_kernel, by_chip=by_chip),
         grid_spec=pltpu.PrefetchScalarGridSpec(
             num_scalar_prefetch=1,
             grid=(steps,),
@@ -353,22 +353,18 @@
     ]
 
     def weight_copies(index, r):
-        column = pl.multiple_of((chip ^ r) * lanes, lanes)
         if index == 0:
             pairs = [(weights[0].at[r], held.at[0, :, pl.ds(r * lanes, lanes)])]
-        elif index == 1:
-            half = depth // 2
+        else:
+            column = pl.multiple_of((chip ^ r) * lanes, lanes)
+            half, first = depth // 2, 5 * index - 4
             pairs = [
                 (
-                    weights[4 + part].at[0] if r == 3 else weights[1 + r].at[part],
-                    held.at[1, pl.ds(part * half, half), pl.ds(column, lanes)],
+                    weights[first + 3 + part].at[0] if r == 3 else weights[first + r].at[part],
+                    held.at[index, pl.ds(part * half, half), pl.ds(column, lanes)],
                 )
                 for part in range(2)
             ]
-        else:
-            part = index - 2
-            source = weights[9 + part].at[0] if r == 3 else weights[6 + r].at[part]
-            pairs = [(source, held.at[index, :, pl.ds(column, lanes)])]
         return [
             pltpu.make_async_copy(source, target, sem_w.at[index, r, number])
             for number, (source, target) in enumerate(pairs)
@@ -483,6 +479,11 @@
     return up, down
 
 
+def z_last_step(z, up, down):
+    out = lax.ppermute(jnp.where(z == 2, up, down), "z", [(2, 3), (1, 0)])
+    return out, out
+
+
 def by_block(z, steps, column):
     up, down = zip(*steps)
     if column == 1:
@@ -546,7 +547,9 @@
     w_own = w_cut[:, : 3 * rows_dev].reshape(groups, 3, rows_dev, cols)
     slot_ids = w_cut[:, 3 * rows_dev, : slots_here.shape[0]].astype(jnp.int32)
     slot_ids = slot_ids.reshape(zs, CORES, REQ, new_dev)[blocks]
-    slot_ids = slot_ids[:, :, chip ^ jnp.arange(REQ)].reshape(zs, CORES, 1, REQ * new_dev)
+    near_first = slot_ids[:2, :, chip ^ jnp.arange(REQ)]
+    slot_ids = jnp.concatenate([near_first, slot_ids[2:]], axis=0)
+    slot_ids = slot_ids.reshape(zs, CORES, 1, REQ * new_dev)
 
     out_parts = [lax.all_gather(w_out, "r", axis=0, tiled=False)]
 
@@ -570,16 +573,17 @@
     w_parts = [w_parts[0], far(w_parts[1])]
     weights = [piece for part in w_parts for piece in part]
 
-    def run(first, pairs, held, cost):
+    def run(first, pairs, held, cost, by_chip):
         steps = len(pairs) // CORES
         place = jnp.concatenate([jnp.stack([chip, core]), blocks[first : first + steps]])
-        *held, fresh = project(pairs, weights, *tables, place.astype(jnp.int32), held, cost)
+        place = place.astype(jnp.int32)
+        *held, fresh = project(pairs, weights, *tables, place, held, cost, by_chip)
         return held, fresh
 
     def send(fresh):
         return [fresh[0]] + [swap_chips(fresh[away], away) for away in range(1, REQ)]
 
-    held, fresh = run(0, [x_own, other_own, x_first, other_first], (), 0)
+    held, fresh = run(0, [x_own, other_own, x_first, other_first], (), 0, False)
     x_steps, held, fresh, x_second, other_second, w_out = lax.optimization_barrier(
         (x_steps, held, fresh, x_second, other_second, w_out)
     )
@@ -587,15 +591,16 @@
     x_last = by_block(z, x_steps, 3)
     sent = send(fresh)
     cached = lax.all_to_all(cut, seq, split_axis=0, concat_axis=0, tiled=True)
-    held, fresh = run(2, [x_second, other_second, x_last, swap_cores(x_last)], held, 1)
+    pairs = [x_second, other_second, x_last, swap_cores(x_last)]
+    held, fresh = run(2, pairs, held, 1, True)
     out_steps, sent, held, fresh, cached = lax.optimization_barrier(
         (out_steps, sent, held, fresh, cached)
     )
     w_first = by_block(z, out_steps, 1)
-    w_first = far(near((w_first.reshape(2, w_first.shape[0] // 2, w_first.shape[1]),)))
+    w_first = near((w_first.reshape(2, w_first.shape[0] // 2, w_first.shape[1]),))
     out_steps += [z_step(*out_steps[0], 1)]
-    out_steps += [z_step(*out_steps[1], 2)]
-    sent += send(fresh)
+    whole = lax.all_to_all(fresh, "r", split_axis=0, concat_axis=0, tiled=True)
+    sent += [whole[r] for r in range(REQ)]
     query, keys, values = held
     flat = (new_len, cols)
 
@@ -605,14 +610,20 @@
     out_steps, attended, sent, w_first = lax.optimization_barrier(
         (out_steps, attended, sent, w_first)
     )
-    out_parts += w_first
-    rest = near((jnp.stack([by_block(z, out_steps, 2), by_block(z, out_steps, 3)]),))
+    out_steps += [z_last_step(z, *out_steps[1])]
     back = lax.all_to_all(
         attended.reshape(seq_count, new_dev, cols), seq, split_axis=0, concat_axis=0, tiled=True
     )
+    w_second = by_block(z, out_steps, 2)
+    w_second = near((w_second.reshape(2, w_second.shape[0] // 2, w_second.shape[1]),))
     outgoing = order(blocks, slot_ids, sent, seq_count)
-    back, outgoing, rest = lax.optimization_barrier((back, outgoing, rest))
-    out_parts += far(rest)
+    out_parts += far(w_first)
+    back, outgoing, out_parts, out_steps, w_second = lax.optimization_barrier(
+        (back, outgoing, out_parts, out_steps, w_second)
+    )
+    out_parts += far(w_second)
+    w_third = by_block(z, out_steps, 3)
+    out_parts += far(near((w_third.reshape(2, w_third.shape[0] // 2, w_third.shape[1]),)))
     arrived = lax.all_to_all(outgoing, seq, split_axis=0, concat_axis=0, tiled=True)
     appended = arrived.reshape(zs, REQ, CORES, zs, CORES, SLOTS, 2, cols)
     appended = appended.transpose(3, 1, 4, 5, 6, 0, 2, 7).reshape(seq_count * SLOTS, 2, width)

time: 609 us -> 596 us (0.979)
  waiting for transfers between devices: 316 us -> 297 us
    ppermute x25 -> x26, waiting for transfers between devices: 260 us -> 242 us  [swap_chips(): lax.ppermute(value, 'r', [(chip, chip ^ away) for chip in range(REQ)])]
    slice x8 -> x10, local copies, waits for them, and re-layouts: 9.08 us -> 12.4 us  [far(): return part + (swap_chips(part[1][:half], 2), swap_chips(part[2][half:], 1))]
    ppermute x25 -> x26, starting transfers between devices: 24.4 us -> 22.4 us  [swap_chips(): lax.ppermute(value, 'r', [(chip, chip ^ away) for chip in range(REQ)])]
    ppermute x6 -> x5, waiting for transfers between devices: 12.3 us -> 10.5 us  [z_step(): up = lax.ppermute(up, 'z', [(z, z + 1) for z in range(step, last)])]
    ppermute x6 -> x5, starting transfers between devices: 16.2 us -> 14.7 us  [z_step(): up = lax.ppermute(up, 'z', [(z, z + 1) for z in range(step, last)])]
    ppermute x6 -> x5, starting transfers between devices: 15.9 us -> 17.1 us  [z_step(): lax.ppermute(down, 'z', [(z, z - 1) for z in range(1, Z_CHIPS - step)])]
    ppermute x6 -> x5, waiting for transfers between devices: 13.3 us -> 13.9 us  [z_step(): lax.ppermute(down, 'z', [(z, z - 1) for z in range(1, Z_CHIPS - step)])]
  transfers between devices with their start and end apart: 48 -> 49, of which waited for: 25 -> 27; matrix products, arithmetic and copies ran while one was open for 6% -> 8% of each run, Pallas kernels for 16% -> 17%
where the time goes in v3:
time: 596 us; the launch traced here: 586 us
  waiting for transfers between devices  297 us (50%)
  Pallas kernels  97.6 us (16%)
  starting transfers between devices  91.8 us (15%)
  local copies, waits for them, and re-layouts  51.2 us (9%)
  other arithmetic  33.7 us (6%)
  between operations  15 us (3%)
    ppermute x26, waiting for transfers between devices, swap_chips(): lax.ppermute(value, 'r', [(chip, chip ^ away) for chip in range(REQ)])  242 us
    pallas_call x2, Pallas kernels, project(): pl.pallas_call(functools.partial(project_kernel, by_chip=by_chip), grid_s...  45 us
    all_to_all x1, waiting for transfers between devices, by_heads(): lax.all_to_all(w_cut, ('z', 'c'), split_axis=0, concat_axis=0, tiled=True)  27.3 us
    pallas_call x1, Pallas kernels, attend(): pl.pallas_call(functools.partial(attend_kernel, blocks=blocks), grid_spec...  25.2 us
    ppermute x26, starting transfers between devices, swap_chips(): lax.ppermute(value, 'r', [(chip, chip ^ away) for chip in range(REQ)])  22.4 us
    pallas_call x1, Pallas kernels, output(): pl.pallas_call(output_kernel, grid_spec=pltpu.PrefetchScalarGridSpec(num_...  18.5 us
    ppermute x5, starting transfers between devices, z_step(): lax.ppermute(down, 'z', [(z, z - 1) for z in range(1, Z_CHIPS - step)])  17.1 us
    ppermute x5, starting transfers between devices, z_step(): up = lax.ppermute(up, 'z', [(z, z + 1) for z in range(step, last)])  14.7 us
  transfers between devices with their start and end apart: 49, of which 27 were waited for; matrix products, arithmetic and copies ran while one was open for 8% of the time, Pallas kernels for 17%

profile of v3, /device:TPU:17, one launch (start us, length us, event | category | flops | bytes accessed | tf_op | source)
XLA Modules:
  0.0 586.1 jit_solution(17062449206567946527)
XLA Ops:
  16.7 5.7 all-to-all-start
  28.1 14.5 %collective-permute-done.2 = bf16[64,4096]{1,0:T(8,128)(2,1)S(1)} collective-permute-done((bf16[64,4096]{1,0:T(8,128)(2,1)S(1)}, bf16[64,4096]{1,0:T(8,128)(2,1)S(1)}, u32[]{:S(2)}, u32[]{:S(2)}) %collective-permute-start.2) | collective-permute-done | bytes 524320 | tf_op jit(solution)/shard_map/ppermute | solution.py:468
  42.6 20.0 %collective-permute-done.1 = bf16[64,4096]{1,0:T(8,128)(2,1)S(1)} collective-permute-done((bf16[64,4096]{1,0:T(8,128)(2,1)S(1)}, bf16[64,4096]{1,0:T(8,128)(2,1)S(1)}, u32[]{:S(2)}, u32[]{:S(2)}) %collective-permute-start.1) | collective-permute-done | bytes 524320 | tf_op jit(solution)/shard_map/ppermute | solution.py:468
  64.2 27.3 %all-to-all-done = bf16[8,392,512]{2,1,0:T(8,128)(2,1)} async-done(((bf16[8,392,512]{2,1,0:T(8,128)(2,1)}), bf16[8,392,512]{2,1,0:T(8,128)(2,1)}, u32[]{:S(2)}, u32[]{:S(2)}) %all-to-all-start) | async-done | bytes 3211296 | tf_op jit(solution)/shard_map/all_to_all | solution.py:525
  113.8 28.1 %collective-permute-done.6.refs_2_ = bf16[8,2,128,512]{3,2,1,0:T(8,128)(2,1)} collective-permute-done((bf16[8,2,128,512]{3,2,1,0:T(8,128)(2,1)}, bf16[8,2,128,512]{3,2,1,0:T(8,128)(2,1)}, u32[]{:S(2)}, u32[]{:S(2)}) %collective-permute-start.6) | collective-permute-done | bytes 2097184 | tf_op jit(solution)/shard_map/ppermute | solution.py:468
  142.8 5.8 collective-permute-done.4
  166.9 12.3 %collective-permute-done.11.refs_4_ = bf16[4,2,128,512]{3,2,1,0:T(8,128)(2,1)S(1)} collective-permute-done((bf16[4,2,128,512]{3,2,1,0:T(8,128)(2,1)S(1)}, bf16[4,2,128,512]{3,2,1,0:T(8,128)(2,1)S(1)}, u32[]{:S(2)}, u32[]{:S(2)}) %collective-permute-start.11) | collective-permute-done | bytes 1048608 | tf_op jit(solution)/shard_map/ppermute | solution.py:468
  181.4 21.0 %collective-permute-done.13.refs_7_ = bf16[8,1,128,512]{3,2,1,0:T(8,128)(2,1)} collective-permute-done((bf16[8,1,128,512]{3,2,1,0:T(8,128)(2,1)S(1)}, bf16[8,1,128,512]{3,2,1,0:T(8,128)(2,1)}, u32[]{:S(2)}, u32[]{:S(2)}) %collective-permute-start.13) | collective-permute-done | bytes 1048608 | tf_op jit(solution)/shard_map/ppermute | solution.py:468
  225.9 10.0 %collective-permute-done.18.refs_9_ = bf16[4,1,128,512]{3,2,1,0:T(8,128)(2,1)S(1)} collective-permute-done((bf16[4,1,128,512]{3,2,1,0:T(8,128)(2,1)}, bf16[4,1,128,512]{3,2,1,0:T(8,128)(2,1)S(1)}, u32[]{:S(2)}, u32[]{:S(2)}) %collective-permute-start.18) | collective-permute-done | bytes 524320 | tf_op jit(solution)/shard_map/ppermute | solution.py:468
  237.6 22.5 %shard_map.104 = (bf16[4,4,2,64,512]{4,3,2,1,0:T(8,128)(2,1)}, bf16[4,4,2,64,512]{4,3,2,1,0:T(8,128)(2,1)}, bf16[4,4,2,64,512]{4,3,2,1,0:T(8,128)(2,1)}, bf16[4,2,2,64,1024]{4,3,2,1,0:T(8,128)(2,1)}) custom-call(s32[4]{0:T(128)} %pad_add_fusion.2.place, bf16[8,2,128,512]{3,2,1,0:T(8,128)(2,1)} %slice.144.refs_0_, ...), custom_call_target="tpu_custom_call" | custom-call | tf_op jit(solution)/shard_map/pallas_call | solution.py:158
  268.1 8.8 %all-to-all-start.1 = ((bf16[32,2,16,512]{3,2,1,0:T(8,128)(2,1)}), bf16[32,2,16,512]{3,2,1,0:T(8,128)(2,1)S(1)}, u32[]{:S(2)}, u32[]{:S(2)}) async-start(bf16[32,2,16,512]{3,2,1,0:T(8,128)(2,1)} %bitcast.25), calls=%async_computation.1 | async-start | bytes 2097152 | tf_op jit(solution)/shard_map/all_to_all | solution.py:593
  287.8 22.5 %shard_map.105 = (bf16[4,4,2,64,512]{4,3,2,1,0:T(8,128)(2,1)}, bf16[4,4,2,64,512]{4,3,2,1,0:T(8,128)(2,1)}, bf16[4,4,2,64,512]{4,3,2,1,0:T(8,128)(2,1)}, bf16[4,2,2,64,1024]{4,3,2,1,0:T(8,128)(2,1)}) custom-call(s32[4]{0:T(128)} %pad_add_fusion.4.place, ...), custom_call_target="tpu_custom_call", output_to_operand_aliasing={{0}: (17, {}), {1}: (18, {}), {2}: (19, {})} | custom-call | flops 12884901888 | bytes 20971520 | tf_op jit(solution)/shard_map/pallas_call | solution.py:158
  310.3 5.8 collective-permute-done.23.refs_2_
  316.2 5.9 %collective-permute-done.21 = bf16[4096,128]{1,0:T(8,128)(2,1)} collective-permute-done((bf16[4096,128]{1,0:T(8,128)(2,1)}, bf16[4096,128]{1,0:T(8,128)(2,1)}, u32[]{:S(2)}, u32[]{:S(2)}) %collective-permute-start.21) | collective-permute-done | bytes 1048608 | tf_op jit(solution)/shard_map/ppermute | solution.py:478
  339.6 25.2 %shard_map.106 = bf16[2048,512]{1,0:T(8,128)(2,1)} custom-call(s32[1]{0:T(128)} %bitcast.26.length, bf16[2048,512]{1,0:T(8,128)(2,1)S(1)} %bitcast.94, bf16[2048,512]{1,0:T(8,128)(2,1)} %bitcast.112, bf16[2048,512]{1,0:T(8,128)(2,1)} %bitcast.113, bf16[32,2,16,512]{3,2,1,0:T(8,128)(2,1)S(1)} %all-to-all-done.1.kc_ref.vc_ref, ...), custom_call_target="tpu_custom_call" | custom-call | flops 6442450944 | bytes 8388608 | tf_op jit(solution)/shard_map/pallas_call | solution.py:304
  366.2 7.6 %collective-permute-done.29.refs_5_ = bf16[2,2048,128]{2,1,0:T(8,128)(2,1)} collective-permute-done((bf16[2,2048,128]{2,1,0:T(8,128)(2,1)}, bf16[2,2048,128]{2,1,0:T(8,128)(2,1)}, u32[]{:S(2)}, u32[]{:S(2)}) %collective-permute-start.29) | collective-permute-done | bytes 1048608 | tf_op jit(solution)/shard_map/ppermute | solution.py:468
  394.7 6.1 %shard_map.107 = bf16[32,4,16,1024]{3,2,1,0:T(8,128)(2,1)} custom-call(s32[4]{0:T(128)} %get-tuple-element.205.blocks, s32[4,2,1,256]{3,2,1,0:T(1,128)} %reshape.282.slot_ref, bf16[2,2,64,1024]{3,2,1,0:T(8,128)(2,1)} %get-tuple-element.156.refs_0_, bf16[2,2,64,1024]{3,2,1,0:T(8,128)(2,1)} %copy-done.13, bf16[2,2,64,1024]{3,2,1,0:T(8,128)(2,1)} %copy-done.12, ...), custom_call_target="tpu_custom_call" | custom-call | flops 1073741824 | bytes 8388608 | tf_op jit(solution)/shard_map/pallas_call | solution.py:223
  400.8 36.5 %collective-permute-done.31.refs_7_ = bf16[1,2048,128]{2,1,0:T(8,128)(2,1)} collective-permute-done((bf16[1,2048,128]{2,1,0:T(8,128)(2,1)}, bf16[1,2048,128]{2,1,0:T(8,128)(2,1)}, u32[]{:S(2)}, u32[]{:S(2)}) %collective-permute-start.31) | collective-permute-done | bytes 524320 | tf_op jit(solution)/shard_map/ppermute | solution.py:468
  450.3 54.3 %collective-permute-done.39.refs_15_ = bf16[2,2048,128]{2,1,0:T(8,128)(2,1)S(1)} collective-permute-done((bf16[2,2048,128]{2,1,0:T(8,128)(2,1)S(1)}, bf16[2,2048,128]{2,1,0:T(8,128)(2,1)S(1)}, u32[]{:S(2)}, u32[]{:S(2)}) %collective-permute-start.39) | collective-permute-done | bytes 1048608 | tf_op jit(solution)/shard_map/ppermute | solution.py:468
  508.2 15.6 %collective-permute-done.37.refs_12_ = bf16[1,2048,128]{2,1,0:T(8,128)(2,1)S(1)} collective-permute-done((bf16[1,2048,128]{2,1,0:T(8,128)(2,1)S(1)}, bf16[1,2048,128]{2,1,0:T(8,128)(2,1)S(1)}, u32[]{:S(2)}, u32[]{:S(2)}) %collective-permute-start.37) | collective-permute-done | bytes 524320 | tf_op jit(solution)/shard_map/ppermute | solution.py:468
  523.9 11.2 %collective-permute-done.41.refs_17_ = bf16[1,2048,128]{2,1,0:T(8,128)(2,1)S(1)} collective-permute-done((bf16[1,2048,128]{2,1,0:T(8,128)(2,1)S(1)}, bf16[1,2048,128]{2,1,0:T(8,128)(2,1)S(1)}, u32[]{:S(2)}, u32[]{:S(2)}) %collective-permute-start.41) | collective-permute-done | bytes 524320 | tf_op jit(solution)/shard_map/ppermute | solution.py:468
  536.7 18.5 %shard_map.108 = (bf16[256,2048]{1,0:T(8,128)(2,1)}, bf16[256,2048]{1,0:T(8,128)(2,1)}) custom-call(s32[5]{0:T(128)} %pad_add_fusion.1.place, bf16[32,64,512]{2,1,0:T(8,128)(2,1)} %copy-done.4, bf16[32,64,512]{2,1,0:T(8,128)(2,1)} %collective-permute-done.35.refs_1_, bf16[4,4096,128]{2,1,0:T(8,128)(2,1)} %bitcast.111, ...), custom_call_target="tpu_custom_call" | custom-call | flops 8589934592 | bytes 20971520 | tf_op jit(solution)/shard_map/pallas_call | solution.py:405
  562.6 8.6 %copy.24 = bf16[4,4,2,8,2,4,2,512]{7,6,5,4,3,2,1,0:T(2,128)(2,1)} copy(bf16[4,4,2,8,2,4,2,512]{7,3,4,2,0,6,1,5:T(8,128)(2,1)} %bitcast.44) | data formatting | bytes 8388608 | tf_op jit(solution)/shard_map/transpose | solution.py:629
  571.2 7.6 %reshape.287 = bf16[256,2,4096]{2,1,0:T(2,128)(2,1)} reshape(bf16[4,4,2,8,2,4,2,512]{7,6,5,4,3,2,1,0:T(2,128)(2,1)} %copy.24) | data formatting | bytes 8388608 | tf_op jit(solution)/shard_map/reshape | solution.py:629
  (202 shorter events, 169.7 us)
Async XLA Ops:
  16.7 74.8 %all-to-all-start = ((bf16[8,392,512]{2,1,0:T(8,128)(2,1)}), bf16[8,392,512]{2,1,0:T(8,128)(2,1)}, u32[]{:S(2)}, u32[]{:S(2)}) async-start(bf16[8,392,512]{2,1,0:T(8,128)(2,1)} %pad_maximum_fusion), calls=%async_computation | async-start | bytes 6422528 | tf_op jit(solution)/shard_map/all_to_all | solution.py:525
  22.3 91.5 %all-gather.3.cloned.1.call-start = ((), (), s32[]{:S(2)}) async-start(), calls=%async_computation.5 | async-start | bytes 5242880 | tf_op jit(solution)/shard_map/all_gather | solution.py:554
  95.2 46.6 %collective-permute-start.6 = (bf16[8,2,128,512]{3,2,1,0:T(8,128)(2,1)}, bf16[8,2,128,512]{3,2,1,0:T(8,128)(2,1)}, u32[]{:S(2)}, u32[]{:S(2)}) collective-permute-start(bf16[8,2,128,512]{3,2,1,0:T(8,128)(2,1)} %slice.144.refs_0_), channel_id=1, source_target_pairs={{0,4},{2,6},{4,0},{6,2},{1,5},{3,7},{5,1},{7,3},{8,12},{10,14},{12... | collective-permute-start | bytes 6291464 | tf_op jit(solution)/shard_map/ppermute | solution.py:468
  96.5 46.3 %collective-permute-start.5 = (bf16[8,2,128,512]{3,2,1,0:T(8,128)(2,1)}, bf16[8,2,128,512]{3,2,1,0:T(8,128)(2,1)}, u32[]{:S(2)}, u32[]{:S(2)}) collective-permute-start(bf16[8,2,128,512]{3,2,1,0:T(8,128)(2,1)} %slice.144.refs_0_), channel_id=1, source_target_pairs={{0,2},{2,0},{4,6},{6,4},{1,3},{3,1},{5,7},{7,5},{8,10},{10,8},{12,... | collective-permute-start | bytes 6291464 | tf_op jit(solution)/shard_map/ppermute | solution.py:468
  99.1 49.5 %collective-permute-start.4 = (bf16[4,64,4096]{2,1,0:T(8,128)(2,1)}, bf16[4,64,4096]{2,1,0:T(8,128)(2,1)}, u32[]{:S(2)}, u32[]{:S(2)}) collective-permute-start(bf16[4,64,4096]{2,1,0:T(8,128)(2,1)} %pad_maximum_fusion.1.refs_12_), channel_id=1, source_target_pairs={{8,0},{16,8},{24,16},{9,1},{17,9},{25,17},{10,2},{18,10},{26,18},{... | collective-permute-start | bytes 6291464 | tf_op jit(solution)/shard_map/ppermute | solution.py:478
  101.1 51.3 %collective-permute-start.3 = (bf16[4,64,4096]{2,1,0:T(8,128)(2,1)}, bf16[4,64,4096]{2,1,0:T(8,128)(2,1)}, u32[]{:S(2)}, u32[]{:S(2)}) collective-permute-start(bf16[4,64,4096]{2,1,0:T(8,128)(2,1)} %pad_maximum_fusion.1.refs_12_), channel_id=1, source_target_pairs={{0,8},{8,16},{16,24},{1,9},{9,17},{17,25},{2,10},{10,18},{18,26},{... | collective-permute-start | bytes 6291464 | tf_op jit(solution)/shard_map/ppermute | solution.py:477
  157.5 46.9 %collective-permute-start.14 = (bf16[4,64,4096]{2,1,0:T(8,128)(2,1)S(1)}, bf16[4,64,4096]{2,1,0:T(8,128)(2,1)}, u32[]{:S(2)}, u32[]{:S(2)}) collective-permute-start(bf16[4,64,4096]{2,1,0:T(8,128)(2,1)S(1)} %broadcast_select_fusion.refs_14_), channel_id=1, source_target_pairs={{0,1},{1,0},{2,3},{3,2},{4,5},{5,4},{6,7},{7,6},{8,9},{9,8},{10,11... | collective-permute-start | bytes 6291464 | tf_op jit(solution)/shard_map/ppermute | solution.py:472
  158.9 49.4 %collective-permute-start.8 = (bf16[4,64,4096]{2,1,0:T(8,128)(2,1)}, bf16[4,64,4096]{2,1,0:T(8,128)(2,1)}, u32[]{:S(2)}, u32[]{:S(2)}) collective-permute-start(bf16[4,64,4096]{2,1,0:T(8,128)(2,1)} %collective-permute-done.3), channel_id=1, source_target_pairs={{8,16},{16,24},{9,17},{17,25},{10,18},{18,26},{11,19},{19,27},{12,... | collective-permute-start | bytes 6291464 | tf_op jit(solution)/shard_map/ppermute | solution.py:477
  161.7 48.9 %collective-permute-start.9 = (bf16[4,64,4096]{2,1,0:T(8,128)(2,1)}, bf16[4,64,4096]{2,1,0:T(8,128)(2,1)}, u32[]{:S(2)}, u32[]{:S(2)}) collective-permute-start(bf16[4,64,4096]{2,1,0:T(8,128)(2,1)} %collective-permute-done.4), channel_id=1, source_target_pairs={{8,0},{16,8},{9,1},{17,9},{10,2},{18,10},{11,3},{19,11},{12,4},{20... | collective-permute-start | bytes 6291464 | tf_op jit(solution)/shard_map/ppermute | solution.py:478
  213.7 46.4 %collective-permute-start.19 = (bf16[4,64,4096]{2,1,0:T(8,128)(2,1)}, bf16[4,64,4096]{2,1,0:T(8,128)(2,1)}, u32[]{:S(2)}, u32[]{:S(2)}) collective-permute-start(bf16[4,64,4096]{2,1,0:T(8,128)(2,1)} %select_select_fusion.1.refs_12_), channel_id=1, source_target_pairs={{0,1},{1,0},{2,3},{3,2},{4,5},{5,4},{6,7},{7,6},{8,9},{9,8},{10,11... | collective-permute-start | bytes 6291464 | tf_op jit(solution)/shard_map/ppermute | solution.py:472
  214.8 46.8 %collective-permute-start.15 = (bf16[4,64,4096]{2,1,0:T(8,128)(2,1)}, bf16[4,64,4096]{2,1,0:T(8,128)(2,1)S(1)}, u32[]{:S(2)}, u32[]{:S(2)}) collective-permute-start(bf16[4,64,4096]{2,1,0:T(8,128)(2,1)} %collective-permute-done.8), channel_id=1, source_target_pairs={{16,24},{17,25},{18,26},{19,27},{20,28},{21,29},{22,30},{23,31}} | collective-permute-start | bytes 6291464 | tf_op jit(solution)/shard_map/ppermute | solution.py:477
  216.3 45.4 %collective-permute-start.16 = (bf16[4,64,4096]{2,1,0:T(8,128)(2,1)}, bf16[4,64,4096]{2,1,0:T(8,128)(2,1)}, u32[]{:S(2)}, u32[]{:S(2)}) collective-permute-start(bf16[4,64,4096]{2,1,0:T(8,128)(2,1)} %collective-permute-done.9), channel_id=1, source_target_pairs={{8,0},{9,1},{10,2},{11,3},{12,4},{13,5},{14,6},{15,7}} | collective-permute-start | bytes 6291464 | tf_op jit(solution)/shard_map/ppermute | solution.py:478
  373.9 63.8 %all-to-all-start.3 = ((bf16[32,64,512]{2,1,0:T(8,128)(2,1)}), bf16[32,64,512]{2,1,0:T(8,128)(2,1)S(1)}, u32[]{:S(2)}, u32[]{:S(2)}) async-start(bf16[32,64,512]{2,1,0:T(8,128)(2,1)} %bitcast.35), calls=%async_computation.3 | async-start | bytes 4194304 | tf_op jit(solution)/shard_map/all_to_all | solution.py:614
  382.3 55.4 %collective-permute-start.34 = (bf16[2,2048,128]{2,1,0:T(8,128)(2,1)}, bf16[2,2048,128]{2,1,0:T(8,128)(2,1)}, u32[]{:S(2)}, u32[]{:S(2)}) collective-permute-start(bf16[2,2048,128]{2,1,0:T(8,128)(2,1)} %bitcast.40.refs_8_), channel_id=1, source_target_pairs={{0,4},{2,6},{4,0},{6,2},{1,5},{3,7},{5,1},{7,3},{8,12},{10,14},{12... | collective-permute-start | bytes 3145736 | tf_op jit(solution)/shard_map/ppermute | solution.py:468
  383.5 54.2 %collective-permute-start.33 = (bf16[2,2048,128]{2,1,0:T(8,128)(2,1)}, bf16[2,2048,128]{2,1,0:T(8,128)(2,1)}, u32[]{:S(2)}, u32[]{:S(2)}) collective-permute-start(bf16[2,2048,128]{2,1,0:T(8,128)(2,1)} %bitcast.40.refs_8_), channel_id=1, source_target_pairs={{0,2},{2,0},{4,6},{6,4},{1,3},{3,1},{5,7},{7,5},{8,10},{10,8},{12,... | collective-permute-start | bytes 3145736 | tf_op jit(solution)/shard_map/ppermute | solution.py:468
  384.7 53.0 %collective-permute-start.32 = (bf16[4096,128]{1,0:T(8,128)(2,1)}, bf16[4096,128]{1,0:T(8,128)(2,1)S(1)}, u32[]{:S(2)}, u32[]{:S(2)}) collective-permute-start(bf16[4096,128]{1,0:T(8,128)(2,1)} %get-tuple-element.189), channel_id=1, source_target_pairs={{16,24},{8,0},{17,25},{9,1},{18,26},{10,2},{19,27},{11,3},{20,28},... | collective-permute-start | bytes 3145736 | tf_op jit(solution)/shard_map/ppermute | solution.py:483
  391.4 45.9 %collective-permute-start.31 = (bf16[1,2048,128]{2,1,0:T(8,128)(2,1)}, bf16[1,2048,128]{2,1,0:T(8,128)(2,1)}, u32[]{:S(2)}, u32[]{:S(2)}) collective-permute-start(bf16[1,2048,128]{2,1,0:T(8,128)(2,1)} %slice.134), channel_id=1, source_target_pairs={{0,2},{2,0},{4,6},{6,4},{1,3},{3,1},{5,7},{7,5},{8,10},{10,8},{12,... | collective-permute-start | bytes 1572872 | tf_op jit(solution)/shard_map/ppermute | solution.py:468
  391.7 46.0 %collective-permute-start.30 = (bf16[1,2048,128]{2,1,0:T(8,128)(2,1)}, bf16[1,2048,128]{2,1,0:T(8,128)(2,1)}, u32[]{:S(2)}, u32[]{:S(2)}) collective-permute-start(bf16[1,2048,128]{2,1,0:T(8,128)(2,1)} %slice.133), channel_id=1, source_target_pairs={{0,4},{2,6},{4,0},{6,2},{1,5},{3,7},{5,1},{7,3},{8,12},{10,14},{12... | collective-permute-start | bytes 1572872 | tf_op jit(solution)/shard_map/ppermute | solution.py:468
  437.7 124.9 %all-to-all-start.4 = ((bf16[32,4,16,1024]{3,2,1,0:T(8,128)(2,1)}), bf16[32,4,16,1024]{3,2,1,0:T(8,128)(2,1)}, u32[]{:S(2)}, u32[]{:S(2)}) async-start(bf16[32,4,16,1024]{3,2,1,0:T(8,128)(2,1)} %shard_map.107), calls=%async_computation.4 | async-start | bytes 8388608 | tf_op jit(solution)/shard_map/all_to_all | solution.py:627
  443.2 93.5 %collective-permute-start.35 = (bf16[32,64,512]{2,1,0:T(8,128)(2,1)S(1)}, bf16[32,64,512]{2,1,0:T(8,128)(2,1)}, u32[]{:S(2)}, u32[]{:S(2)}) collective-permute-start(bf16[32,64,512]{2,1,0:T(8,128)(2,1)S(1)} %all-to-all-done.3.refs_0_), channel_id=1, source_target_pairs={{0,1},{1,0},{2,3},{3,2},{4,5},{5,4},{6,7},{7,6},{8,9},{9,8},{10,11... | collective-permute-start | bytes 6291464 | tf_op jit(solution)/shard_map/ppermute | solution.py:472
  445.0 59.5 %collective-permute-start.39 = (bf16[2,2048,128]{2,1,0:T(8,128)(2,1)S(1)}, bf16[2,2048,128]{2,1,0:T(8,128)(2,1)S(1)}, u32[]{:S(2)}, u32[]{:S(2)}) collective-permute-start(bf16[2,2048,128]{2,1,0:T(8,128)(2,1)S(1)} %bitcast.101), channel_id=1, source_target_pairs={{0,4},{2,6},{4,0},{6,2},{1,5},{3,7},{5,1},{7,3},{8,12},{10,14},{12... | collective-permute-start | bytes 3145736 | tf_op jit(solution)/shard_map/ppermute | solution.py:468
  446.3 59.9 %collective-permute-start.38 = (bf16[2,2048,128]{2,1,0:T(8,128)(2,1)S(1)}, bf16[2,2048,128]{2,1,0:T(8,128)(2,1)S(1)}, u32[]{:S(2)}, u32[]{:S(2)}) collective-permute-start(bf16[2,2048,128]{2,1,0:T(8,128)(2,1)S(1)} %bitcast.102), channel_id=1, source_target_pairs={{0,2},{2,0},{4,6},{6,4},{1,3},{3,1},{5,7},{7,5},{8,10},{10,8},{12,... | collective-permute-start | bytes 3145736 | tf_op jit(solution)/shard_map/ppermute | solution.py:468
  449.7 74.2 %collective-permute-start.37 = (bf16[1,2048,128]{2,1,0:T(8,128)(2,1)S(1)}, bf16[1,2048,128]{2,1,0:T(8,128)(2,1)S(1)}, u32[]{:S(2)}, u32[]{:S(2)}) collective-permute-start(bf16[1,2048,128]{2,1,0:T(8,128)(2,1)S(1)} %slice.136), channel_id=1, source_target_pairs={{0,2},{2,0},{4,6},{6,4},{1,3},{3,1},{5,7},{7,5},{8,10},{10,8},{12,... | collective-permute-start | bytes 1572872 | tf_op jit(solution)/shard_map/ppermute | solution.py:468
  450.0 73.9 %collective-permute-start.36 = (bf16[1,2048,128]{2,1,0:T(8,128)(2,1)S(1)}, bf16[1,2048,128]{2,1,0:T(8,128)(2,1)S(1)}, u32[]{:S(2)}, u32[]{:S(2)}) collective-permute-start(bf16[1,2048,128]{2,1,0:T(8,128)(2,1)S(1)} %slice.135), channel_id=1, source_target_pairs={{0,4},{2,6},{4,0},{6,2},{1,5},{3,7},{5,1},{7,3},{8,12},{10,14},{12... | collective-permute-start | bytes 1572872 | tf_op jit(solution)/shard_map/ppermute | solution.py:468
  (52 other events, 1158.9 us)
Sparse Core Ops, SparseCore 0:
  25.0 68.1 all-gather.2

commit v4 on v3

--- a/solution.py
+++ b/solution.py
@@ -327,9 +327,10 @@
     )(jnp.reshape(length, (1,)), query, keys, values, cached, cached)
 
 
-def output_kernel(place, *refs):
+def output_kernel(place, *refs, pieces, whole):
     mine_ref, other_ref, lhs, held, sem_l, sem_w = refs[-6:]
-    sources, weights = refs[:CORES], refs[CORES:-6]
+    sources, weights = refs[:CORES], refs[CORES : CORES + pieces]
+    steps = held.shape[0]
     zs = lhs.shape[3] // (sources[0].shape[2] * CORES)
     each, cols = sources[0].shape[1:]
     lanes = weights[0].shape[2]
@@ -353,11 +354,11 @@
     ]
 
     def weight_copies(index, r):
-        if index == 0:
-            pairs = [(weights[0].at[r], held.at[0, :, pl.ds(r * lanes, lanes)])]
+        if index < whole:
+            pairs = [(weights[index].at[r], held.at[index, :, pl.ds(r * lanes, lanes)])]
         else:
             column = pl.multiple_of((chip ^ r) * lanes, lanes)
-            half, first = depth // 2, 5 * index - 4
+            half, first = depth // 2, 5 * index - 4 * whole
             pairs = [
                 (
                     weights[first + 3 + part].at[0] if r == 3 else weights[first + r].at[part],
@@ -374,14 +375,14 @@
     def _():
         for part in row_parts:
             row_copy(*part).start()
-        for index in range(zs):
+        for index in range(steps):
             for r in range(REQ):
                 for copy in weight_copies(index, r):
                     copy.start()
         for part in row_parts:
             row_copy(*part).wait()
 
-    for index in range(zs):
+    for index in range(steps):
 
         @pl.when(step == index)
         def _(index=index):
@@ -395,37 +396,39 @@
     other_ref[...] = out[REQ * each :]
 
 
-def output(place, back, back_other, weights):
+def output(place, back, back_other, weights, whole, held):
     sources, each, cols = back.shape
-    _, depth, lanes = weights[0].shape
+    lanes, depth = weights[0].shape[2], sources // REQ * cols
     zs = sources // (REQ * CORES)
+    steps = whole + (len(weights) - whole) // 5
     anywhere = pl.BlockSpec(memory_space=pl.ANY)
     block = pl.BlockSpec((REQ * each, REQ * lanes), lambda i, s: (0, s[1 + i]))
     shape = jax.ShapeDtypeStruct((REQ * each, zs * REQ * lanes), jnp.bfloat16)
     return pl.pallas_call(
-        output_kernel,
+        functools.partial(output_kernel, pieces=len(weights), whole=whole),
         grid_spec=pltpu.PrefetchScalarGridSpec(
             num_scalar_prefetch=1,
-            grid=(zs,),
-            in_specs=[anywhere] * (CORES + len(weights)),
+            grid=(steps,),
+            in_specs=[anywhere] * (CORES + len(weights) + len(held)),
             out_specs=[block, block],
             scratch_shapes=[
                 pltpu.VMEM((CORES, REQ, each, depth), jnp.bfloat16),
-                pltpu.VMEM((zs, depth, REQ * lanes), jnp.bfloat16),
+                pltpu.VMEM((steps, depth, REQ * lanes), jnp.bfloat16),
                 pltpu.SemaphoreType.DMA((CORES, sources)),
-                pltpu.SemaphoreType.DMA((zs, REQ, 2)),
+                pltpu.SemaphoreType.DMA((steps, REQ, 2)),
             ],
         ),
         out_shape=[shape, shape],
+        input_output_aliases={1 + CORES + len(weights) + i: i for i in range(len(held))},
         compiler_params=pltpu.CompilerParams(
             vmem_limit_bytes=56 * 2**20, dimension_semantics=("arbitrary",)
         ),
         cost_estimate=pl.CostEstimate(
-            flops=2 * CORES * REQ * each * depth * zs * REQ * lanes,
-            bytes_accessed=2 * (2 * back.size + depth * zs * REQ * lanes),
+            flops=2 * CORES * REQ * each * depth * steps * REQ * lanes,
+            bytes_accessed=2 * (2 * back.size + depth * steps * REQ * lanes),
             transcendentals=0,
         ),
-    )(place, back, back_other, *weights)
+    )(place, back, back_other, *weights, *held)
 
 
 def interleave_kernel(place, mine_ref, other_ref, out_ref):
@@ -629,7 +632,10 @@
     appended = appended.transpose(3, 1, 4, 5, 6, 0, 2, 7).reshape(seq_count * SLOTS, 2, width)
 
     place = jnp.concatenate([jnp.stack([chip]), blocks]).astype(jnp.int32)
-    out, out_other = output(place, back, swap_cores(back), out_parts)
+    back_other = swap_cores(back)
+    outs = output(place[: zs], back, back_other, out_parts[:-5], 1, ())
+    last = jnp.concatenate([place[:1], place[zs:]])
+    out, out_other = output(last, back, back_other, out_parts[-5:], 0, outs)
     out = interleave(core, out, swap_cores(out_other))
     return out.reshape(REQ, new_dev, out.shape[1]), appended
 

time: 596 us -> 590 us (0.990)
  waiting for transfers between devices: 297 us -> 283 us
    ppermute x26, waiting for transfers between devices: 242 us -> 228 us  [swap_chips(): lax.ppermute(value, 'r', [(chip, chip ^ away) for chip in range(REQ)])]
    pallas_call x1 -> x2, Pallas kernels: 18.5 us -> 22.8 us  [output(): pl.pallas_call(functools.partial(output_kernel, pieces=len(weights), whol...]
  transfers between devices with their start and end apart: 49 -> 49, of which waited for: 27 -> 25; matrix products, arithmetic and copies ran while one was open for 8% -> 8% of each run, Pallas kernels for 17% -> 18%
where the time goes in v4:
time: 590 us; the launch traced here: 581 us
  waiting for transfers between devices  283 us (48%)
  Pallas kernels  102 us (17%)
  starting transfers between devices  92.2 us (16%)
  local copies, waits for them, and re-layouts  53.9 us (9%)
  other arithmetic  35 us (6%)
  between operations  15.1 us (3%)
    ppermute x26, waiting for transfers between devices, swap_chips(): lax.ppermute(value, 'r', [(chip, chip ^ away) for chip in range(REQ)])  228 us
    pallas_call x2, Pallas kernels, project(): pl.pallas_call(functools.partial(project_kernel, by_chip=by_chip), grid_s...  45.1 us
    all_to_all x1, waiting for transfers between devices, by_heads(): lax.all_to_all(w_cut, ('z', 'c'), split_axis=0, concat_axis=0, tiled=True)  27.3 us
    pallas_call x1, Pallas kernels, attend(): pl.pallas_call(functools.partial(attend_kernel, blocks=blocks), grid_spec...  25.3 us
    pallas_call x2, Pallas kernels, output(): pl.pallas_call(functools.partial(output_kernel, pieces=len(weights), whol...  22.8 us
    ppermute x26, starting transfers between devices, swap_chips(): lax.ppermute(value, 'r', [(chip, chip ^ away) for chip in range(REQ)])  22.4 us
    ppermute x5, starting transfers between devices, z_step(): lax.ppermute(down, 'z', [(z, z - 1) for z in range(1, Z_CHIPS - step)])  17 us
    ppermute x5, starting transfers between devices, z_step(): up = lax.ppermute(up, 'z', [(z, z + 1) for z in range(step, last)])  14.7 us
  transfers between devices with their start and end apart: 49, of which 25 were waited for; matrix products, arithmetic and copies ran while one was open for 8% of the time, Pallas kernels for 18%

profile of v4, /device:TPU:17, one launch (start us, length us, event | category | flops | bytes accessed | tf_op | source)
XLA Modules:
  0.0 581.5 jit_solution(8866424978531310735)
XLA Ops:
  16.7 5.7 all-to-all-start
  28.1 14.5 %collective-permute-done.2 = bf16[64,4096]{1,0:T(8,128)(2,1)S(1)} collective-permute-done((bf16[64,4096]{1,0:T(8,128)(2,1)S(1)}, bf16[64,4096]{1,0:T(8,128)(2,1)S(1)}, u32[]{:S(2)}, u32[]{:S(2)}) %collective-permute-start.2) | collective-permute-done | bytes 524320 | tf_op jit(solution)/shard_map/ppermute | solution.py:471
  42.6 20.0 %collective-permute-done.1 = bf16[64,4096]{1,0:T(8,128)(2,1)S(1)} collective-permute-done((bf16[64,4096]{1,0:T(8,128)(2,1)S(1)}, bf16[64,4096]{1,0:T(8,128)(2,1)S(1)}, u32[]{:S(2)}, u32[]{:S(2)}) %collective-permute-start.1) | collective-permute-done | bytes 524320 | tf_op jit(solution)/shard_map/ppermute | solution.py:471
  64.2 27.3 %all-to-all-done = bf16[8,392,512]{2,1,0:T(8,128)(2,1)} async-done(((bf16[8,392,512]{2,1,0:T(8,128)(2,1)}), bf16[8,392,512]{2,1,0:T(8,128)(2,1)}, u32[]{:S(2)}, u32[]{:S(2)}) %all-to-all-start) | async-done | bytes 3211296 | tf_op jit(solution)/shard_map/all_to_all | solution.py:528
  113.9 27.9 %collective-permute-done.6.refs_2_ = bf16[8,2,128,512]{3,2,1,0:T(8,128)(2,1)} collective-permute-done((bf16[8,2,128,512]{3,2,1,0:T(8,128)(2,1)}, bf16[8,2,128,512]{3,2,1,0:T(8,128)(2,1)}, u32[]{:S(2)}, u32[]{:S(2)}) %collective-permute-start.6) | collective-permute-done | bytes 2097184 | tf_op jit(solution)/shard_map/ppermute | solution.py:471
  142.8 5.8 collective-permute-done.4
  166.9 12.3 %collective-permute-done.11.refs_4_ = bf16[4,2,128,512]{3,2,1,0:T(8,128)(2,1)S(1)} collective-permute-done((bf16[4,2,128,512]{3,2,1,0:T(8,128)(2,1)S(1)}, bf16[4,2,128,512]{3,2,1,0:T(8,128)(2,1)S(1)}, u32[]{:S(2)}, u32[]{:S(2)}) %collective-permute-start.11) | collective-permute-done | bytes 1048608 | tf_op jit(solution)/shard_map/ppermute | solution.py:471
  181.5 20.9 %collective-permute-done.13.refs_7_ = bf16[8,1,128,512]{3,2,1,0:T(8,128)(2,1)} collective-permute-done((bf16[8,1,128,512]{3,2,1,0:T(8,128)(2,1)S(1)}, bf16[8,1,128,512]{3,2,1,0:T(8,128)(2,1)}, u32[]{:S(2)}, u32[]{:S(2)}) %collective-permute-start.13) | collective-permute-done | bytes 1048608 | tf_op jit(solution)/shard_map/ppermute | solution.py:471
  225.9 10.0 %collective-permute-done.18.refs_9_ = bf16[4,1,128,512]{3,2,1,0:T(8,128)(2,1)S(1)} collective-permute-done((bf16[4,1,128,512]{3,2,1,0:T(8,128)(2,1)}, bf16[4,1,128,512]{3,2,1,0:T(8,128)(2,1)S(1)}, u32[]{:S(2)}, u32[]{:S(2)}) %collective-permute-start.18) | collective-permute-done | bytes 524320 | tf_op jit(solution)/shard_map/ppermute | solution.py:471
  237.6 22.6 %shard_map.104 = (bf16[4,4,2,64,512]{4,3,2,1,0:T(8,128)(2,1)}, bf16[4,4,2,64,512]{4,3,2,1,0:T(8,128)(2,1)}, bf16[4,4,2,64,512]{4,3,2,1,0:T(8,128)(2,1)}, bf16[4,2,2,64,1024]{4,3,2,1,0:T(8,128)(2,1)}) custom-call(s32[4]{0:T(128)} %pad_add_fusion.2.place, bf16[8,2,128,512]{3,2,1,0:T(8,128)(2,1)} %slice.156.refs_0_, ...), custom_call_target="tpu_custom_call" | custom-call | tf_op jit(solution)/shard_map/pallas_call | solution.py:158
  268.1 8.8 %all-to-all-start.1 = ((bf16[32,2,16,512]{3,2,1,0:T(8,128)(2,1)}), bf16[32,2,16,512]{3,2,1,0:T(8,128)(2,1)S(1)}, u32[]{:S(2)}, u32[]{:S(2)}) async-start(bf16[32,2,16,512]{3,2,1,0:T(8,128)(2,1)} %bitcast.25), calls=%async_computation.1 | async-start | bytes 2097152 | tf_op jit(solution)/shard_map/all_to_all | solution.py:596
  287.8 22.5 %shard_map.105 = (bf16[4,4,2,64,512]{4,3,2,1,0:T(8,128)(2,1)}, bf16[4,4,2,64,512]{4,3,2,1,0:T(8,128)(2,1)}, bf16[4,4,2,64,512]{4,3,2,1,0:T(8,128)(2,1)}, bf16[4,2,2,64,1024]{4,3,2,1,0:T(8,128)(2,1)}) custom-call(s32[4]{0:T(128)} %pad_add_fusion.4.place, ...), custom_call_target="tpu_custom_call", output_to_operand_aliasing={{0}: (17, {}), {1}: (18, {}), {2}: (19, {})} | custom-call | flops 12884901888 | bytes 20971520 | tf_op jit(solution)/shard_map/pallas_call | solution.py:158
  310.3 5.8 %collective-permute-done.23.refs_2_ = bf16[2,2,64,1024]{3,2,1,0:T(8,128)(2,1)S(1)} collective-permute-done((bf16[2,2,64,1024]{3,2,1,0:T(8,128)(2,1)}, bf16[2,2,64,1024]{3,2,1,0:T(8,128)(2,1)S(1)}, u32[]{:S(2)}, u32[]{:S(2)}) %collective-permute-start.23) | collective-permute-done | bytes 524320 | tf_op jit(solution)/shard_map/ppermute | solution.py:471
  316.2 5.9 %collective-permute-done.21 = bf16[4096,128]{1,0:T(8,128)(2,1)} collective-permute-done((bf16[4096,128]{1,0:T(8,128)(2,1)}, bf16[4096,128]{1,0:T(8,128)(2,1)}, u32[]{:S(2)}, u32[]{:S(2)}) %collective-permute-start.21) | collective-permute-done | bytes 1048608 | tf_op jit(solution)/shard_map/ppermute | solution.py:481
  339.5 25.3 %shard_map.106 = bf16[2048,512]{1,0:T(8,128)(2,1)} custom-call(s32[1]{0:T(128)} %bitcast.26.length, bf16[2048,512]{1,0:T(8,128)(2,1)S(1)} %bitcast.96, bf16[2048,512]{1,0:T(8,128)(2,1)} %bitcast.114, bf16[2048,512]{1,0:T(8,128)(2,1)} %bitcast.115, bf16[32,2,16,512]{3,2,1,0:T(8,128)(2,1)S(1)} %all-to-all-done.1.kc_ref.vc_ref, ...), custom_call_target="tpu_custom_call" | custom-call | flops 6442450944 | bytes 8388608 | tf_op jit(solution)/shard_map/pallas_call | solution.py:304
  366.2 7.7 %collective-permute-done.29.refs_5_ = bf16[2,2048,128]{2,1,0:T(8,128)(2,1)} collective-permute-done((bf16[2,2048,128]{2,1,0:T(8,128)(2,1)}, bf16[2,2048,128]{2,1,0:T(8,128)(2,1)}, u32[]{:S(2)}, u32[]{:S(2)}) %collective-permute-start.29) | collective-permute-done | bytes 1048608 | tf_op jit(solution)/shard_map/ppermute | solution.py:471
  394.6 6.1 %shard_map.107 = bf16[32,4,16,1024]{3,2,1,0:T(8,128)(2,1)} custom-call(s32[4]{0:T(128)} %get-tuple-element.208.blocks, s32[4,2,1,256]{3,2,1,0:T(1,128)} %reshape.283.slot_ref, bf16[2,2,64,1024]{3,2,1,0:T(8,128)(2,1)} %get-tuple-element.158.refs_0_, bf16[2,2,64,1024]{3,2,1,0:T(8,128)(2,1)} %copy-done.16, bf16[2,2,64,1024]{3,2,1,0:T(8,128)(2,1)} %copy-done.15, ...), custom_call_target="tpu_custom_call" | custom-call | flops 1073741824 | bytes 8388608 | tf_op jit(solution)/shard_map/pallas_call | solution.py:223
  400.7 36.5 %collective-permute-done.31.refs_7_ = bf16[1,2048,128]{2,1,0:T(8,128)(2,1)} collective-permute-done((bf16[1,2048,128]{2,1,0:T(8,128)(2,1)}, bf16[1,2048,128]{2,1,0:T(8,128)(2,1)}, u32[]{:S(2)}, u32[]{:S(2)}) %collective-permute-start.31) | collective-permute-done | bytes 524320 | tf_op jit(solution)/shard_map/ppermute | solution.py:471
  452.9 51.7 %collective-permute-done.37.refs_4_ = bf16[2,2048,128]{2,1,0:T(8,128)(2,1)S(1)} collective-permute-done((bf16[2,2048,128]{2,1,0:T(8,128)(2,1)S(1)}, bf16[2,2048,128]{2,1,0:T(8,128)(2,1)S(1)}, u32[]{:S(2)}, u32[]{:S(2)}) %collective-permute-start.37) | collective-permute-done | bytes 1048608 | tf_op jit(solution)/shard_map/ppermute | solution.py:471
  507.6 16.3 %collective-permute-done.41.refs_12_ = bf16[1,2048,128]{2,1,0:T(8,128)(2,1)S(1)} collective-permute-done((bf16[1,2048,128]{2,1,0:T(8,128)(2,1)S(1)}, bf16[1,2048,128]{2,1,0:T(8,128)(2,1)S(1)}, u32[]{:S(2)}, u32[]{:S(2)}) %collective-permute-start.41) | collective-permute-done | bytes 524320 | tf_op jit(solution)/shard_map/ppermute | solution.py:471
  526.2 15.0 %shard_map.108 = (bf16[256,2048]{1,0:T(8,128)(2,1)}, bf16[256,2048]{1,0:T(8,128)(2,1)}) custom-call(s32[4]{0:T(128)} %bitcast.116, bf16[32,64,512]{2,1,0:T(8,128)(2,1)} %copy-done.3, bf16[32,64,512]{2,1,0:T(8,128)(2,1)} %copy-done.9, bf16[4,4096,128]{2,1,0:T(8,128)(2,1)} %bitcast.113, bf16[2,2048,128]{2,1,0:T(8,128)(2,1)} %bitcast.34.refs_3_, ...), custom_call_target="tpu_custom_call" | custom-call | flops 6442450944 | bytes 16777216 | tf_op jit(solution)/shard_map/pallas_call | solution.py:407
  542.2 7.9 %shard_map.109 = (bf16[256,2048]{1,0:T(8,128)(2,1)}, bf16[256,2048]{1,0:T(8,128)(2,1)}) custom-call(s32[2]{0:T(128)} %pad_add_fusion.1.place, bf16[32,64,512]{2,1,0:T(8,128)(2,1)} %copy-done.3, bf16[32,64,512]{2,1,0:T(8,128)(2,1)} %copy-done.9, bf16[2,2048,128]{2,1,0:T(8,128)(2,1)} %bitcast.103, ...), custom_call_target="tpu_custom_call", output_to_operand_aliasing={{0}: (8, {}), {1}: (9, {})} | custom-call | flops 2147483648 | bytes 8388608 | tf_op jit(solution)/shard_map/pallas_call | solution.py:407
  558.0 8.6 %copy.26 = bf16[4,4,2,8,2,4,2,512]{7,6,5,4,3,2,1,0:T(2,128)(2,1)} copy(bf16[4,4,2,8,2,4,2,512]{7,3,4,2,0,6,1,5:T(8,128)(2,1)} %bitcast.45) | data formatting | bytes 8388608 | tf_op jit(solution)/shard_map/transpose | solution.py:632
  566.6 7.6 %reshape.288 = bf16[256,2,4096]{2,1,0:T(2,128)(2,1)} reshape(bf16[4,4,2,8,2,4,2,512]{7,6,5,4,3,2,1,0:T(2,128)(2,1)} %copy.26) | data formatting | bytes 8388608 | tf_op jit(solution)/shard_map/reshape | solution.py:632
  (207 shorter events, 173.8 us)
Async XLA Ops:
  16.7 74.8 %all-to-all-start = ((bf16[8,392,512]{2,1,0:T(8,128)(2,1)}), bf16[8,392,512]{2,1,0:T(8,128)(2,1)}, u32[]{:S(2)}, u32[]{:S(2)}) async-start(bf16[8,392,512]{2,1,0:T(8,128)(2,1)} %pad_maximum_fusion), calls=%async_computation | async-start | bytes 6422528 | tf_op jit(solution)/shard_map/all_to_all | solution.py:528
  22.3 91.6 %all-gather.3.cloned.1.call-start = ((), (), s32[]{:S(2)}) async-start(), calls=%async_computation.5 | async-start | bytes 5242880 | tf_op jit(solution)/shard_map/all_gather | solution.py:557
  95.2 46.6 %collective-permute-start.6 = (bf16[8,2,128,512]{3,2,1,0:T(8,128)(2,1)}, bf16[8,2,128,512]{3,2,1,0:T(8,128)(2,1)}, u32[]{:S(2)}, u32[]{:S(2)}) collective-permute-start(bf16[8,2,128,512]{3,2,1,0:T(8,128)(2,1)} %slice.156.refs_0_), channel_id=1, source_target_pairs={{0,4},{2,6},{4,0},{6,2},{1,5},{3,7},{5,1},{7,3},{8,12},{10,14},{12... | collective-permute-start | bytes 6291464 | tf_op jit(solution)/shard_map/ppermute | solution.py:471
  96.5 46.3 %collective-permute-start.5 = (bf16[8,2,128,512]{3,2,1,0:T(8,128)(2,1)}, bf16[8,2,128,512]{3,2,1,0:T(8,128)(2,1)}, u32[]{:S(2)}, u32[]{:S(2)}) collective-permute-start(bf16[8,2,128,512]{3,2,1,0:T(8,128)(2,1)} %slice.156.refs_0_), channel_id=1, source_target_pairs={{0,2},{2,0},{4,6},{6,4},{1,3},{3,1},{5,7},{7,5},{8,10},{10,8},{12,... | collective-permute-start | bytes 6291464 | tf_op jit(solution)/shard_map/ppermute | solution.py:471
  99.1 49.5 %collective-permute-start.4 = (bf16[4,64,4096]{2,1,0:T(8,128)(2,1)}, bf16[4,64,4096]{2,1,0:T(8,128)(2,1)}, u32[]{:S(2)}, u32[]{:S(2)}) collective-permute-start(bf16[4,64,4096]{2,1,0:T(8,128)(2,1)} %pad_maximum_fusion.1.refs_12_), channel_id=1, source_target_pairs={{8,0},{16,8},{24,16},{9,1},{17,9},{25,17},{10,2},{18,10},{26,18},{... | collective-permute-start | bytes 6291464 | tf_op jit(solution)/shard_map/ppermute | solution.py:481
  101.1 51.3 %collective-permute-start.3 = (bf16[4,64,4096]{2,1,0:T(8,128)(2,1)}, bf16[4,64,4096]{2,1,0:T(8,128)(2,1)}, u32[]{:S(2)}, u32[]{:S(2)}) collective-permute-start(bf16[4,64,4096]{2,1,0:T(8,128)(2,1)} %pad_maximum_fusion.1.refs_12_), channel_id=1, source_target_pairs={{0,8},{8,16},{16,24},{1,9},{9,17},{17,25},{2,10},{10,18},{18,26},{... | collective-permute-start | bytes 6291464 | tf_op jit(solution)/shard_map/ppermute | solution.py:480
  157.5 46.9 %collective-permute-start.14 = (bf16[4,64,4096]{2,1,0:T(8,128)(2,1)S(1)}, bf16[4,64,4096]{2,1,0:T(8,128)(2,1)}, u32[]{:S(2)}, u32[]{:S(2)}) collective-permute-start(bf16[4,64,4096]{2,1,0:T(8,128)(2,1)S(1)} %broadcast_select_fusion.refs_14_), channel_id=1, source_target_pairs={{0,1},{1,0},{2,3},{3,2},{4,5},{5,4},{6,7},{7,6},{8,9},{9,8},{10,11... | collective-permute-start | bytes 6291464 | tf_op jit(solution)/shard_map/ppermute | solution.py:475
  158.9 49.4 %collective-permute-start.8 = (bf16[4,64,4096]{2,1,0:T(8,128)(2,1)}, bf16[4,64,4096]{2,1,0:T(8,128)(2,1)}, u32[]{:S(2)}, u32[]{:S(2)}) collective-permute-start(bf16[4,64,4096]{2,1,0:T(8,128)(2,1)} %collective-permute-done.3), channel_id=1, source_target_pairs={{8,16},{16,24},{9,17},{17,25},{10,18},{18,26},{11,19},{19,27},{12,... | collective-permute-start | bytes 6291464 | tf_op jit(solution)/shard_map/ppermute | solution.py:480
  161.6 48.9 %collective-permute-start.9 = (bf16[4,64,4096]{2,1,0:T(8,128)(2,1)}, bf16[4,64,4096]{2,1,0:T(8,128)(2,1)}, u32[]{:S(2)}, u32[]{:S(2)}) collective-permute-start(bf16[4,64,4096]{2,1,0:T(8,128)(2,1)} %collective-permute-done.4), channel_id=1, source_target_pairs={{8,0},{16,8},{9,1},{17,9},{10,2},{18,10},{11,3},{19,11},{12,4},{20... | collective-permute-start | bytes 6291464 | tf_op jit(solution)/shard_map/ppermute | solution.py:481
  213.7 46.5 %collective-permute-start.19 = (bf16[4,64,4096]{2,1,0:T(8,128)(2,1)}, bf16[4,64,4096]{2,1,0:T(8,128)(2,1)}, u32[]{:S(2)}, u32[]{:S(2)}) collective-permute-start(bf16[4,64,4096]{2,1,0:T(8,128)(2,1)} %select_select_fusion.1.refs_12_), channel_id=1, source_target_pairs={{0,1},{1,0},{2,3},{3,2},{4,5},{5,4},{6,7},{7,6},{8,9},{9,8},{10,11... | collective-permute-start | bytes 6291464 | tf_op jit(solution)/shard_map/ppermute | solution.py:475
  214.8 46.8 %collective-permute-start.15 = (bf16[4,64,4096]{2,1,0:T(8,128)(2,1)}, bf16[4,64,4096]{2,1,0:T(8,128)(2,1)S(1)}, u32[]{:S(2)}, u32[]{:S(2)}) collective-permute-start(bf16[4,64,4096]{2,1,0:T(8,128)(2,1)} %collective-permute-done.8), channel_id=1, source_target_pairs={{16,24},{17,25},{18,26},{19,27},{20,28},{21,29},{22,30},{23,31}} | collective-permute-start | bytes 6291464 | tf_op jit(solution)/shard_map/ppermute | solution.py:480
  216.2 45.4 %collective-permute-start.16 = (bf16[4,64,4096]{2,1,0:T(8,128)(2,1)}, bf16[4,64,4096]{2,1,0:T(8,128)(2,1)}, u32[]{:S(2)}, u32[]{:S(2)}) collective-permute-start(bf16[4,64,4096]{2,1,0:T(8,128)(2,1)} %collective-permute-done.9), channel_id=1, source_target_pairs={{8,0},{9,1},{10,2},{11,3},{12,4},{13,5},{14,6},{15,7}} | collective-permute-start | bytes 6291464 | tf_op jit(solution)/shard_map/ppermute | solution.py:481
  373.9 63.8 %all-to-all-start.3 = ((bf16[32,64,512]{2,1,0:T(8,128)(2,1)}), bf16[32,64,512]{2,1,0:T(8,128)(2,1)S(1)}, u32[]{:S(2)}, u32[]{:S(2)}) async-start(bf16[32,64,512]{2,1,0:T(8,128)(2,1)} %bitcast.35), calls=%async_computation.3 | async-start | bytes 4194304 | tf_op jit(solution)/shard_map/all_to_all | solution.py:617
  382.3 55.4 %collective-permute-start.34 = (bf16[2,2048,128]{2,1,0:T(8,128)(2,1)}, bf16[2,2048,128]{2,1,0:T(8,128)(2,1)}, u32[]{:S(2)}, u32[]{:S(2)}) collective-permute-start(bf16[2,2048,128]{2,1,0:T(8,128)(2,1)} %bitcast.41.refs_8_), channel_id=1, source_target_pairs={{0,4},{2,6},{4,0},{6,2},{1,5},{3,7},{5,1},{7,3},{8,12},{10,14},{12... | collective-permute-start | bytes 3145736 | tf_op jit(solution)/shard_map/ppermute | solution.py:471
  383.5 54.2 %collective-permute-start.33 = (bf16[2,2048,128]{2,1,0:T(8,128)(2,1)}, bf16[2,2048,128]{2,1,0:T(8,128)(2,1)}, u32[]{:S(2)}, u32[]{:S(2)}) collective-permute-start(bf16[2,2048,128]{2,1,0:T(8,128)(2,1)} %bitcast.41.refs_8_), channel_id=1, source_target_pairs={{0,2},{2,0},{4,6},{6,4},{1,3},{3,1},{5,7},{7,5},{8,10},{10,8},{12,... | collective-permute-start | bytes 3145736 | tf_op jit(solution)/shard_map/ppermute | solution.py:471
  384.7 53.0 %collective-permute-start.32 = (bf16[4096,128]{1,0:T(8,128)(2,1)}, bf16[4096,128]{1,0:T(8,128)(2,1)S(1)}, u32[]{:S(2)}, u32[]{:S(2)}) collective-permute-start(bf16[4096,128]{1,0:T(8,128)(2,1)} %get-tuple-element.193), channel_id=1, source_target_pairs={{16,24},{8,0},{17,25},{9,1},{18,26},{10,2},{19,27},{11,3},{20,28},... | collective-permute-start | bytes 3145736 | tf_op jit(solution)/shard_map/ppermute | solution.py:486
  391.3 45.9 %collective-permute-start.31 = (bf16[1,2048,128]{2,1,0:T(8,128)(2,1)}, bf16[1,2048,128]{2,1,0:T(8,128)(2,1)}, u32[]{:S(2)}, u32[]{:S(2)}) collective-permute-start(bf16[1,2048,128]{2,1,0:T(8,128)(2,1)} %slice.145), channel_id=1, source_target_pairs={{0,2},{2,0},{4,6},{6,4},{1,3},{3,1},{5,7},{7,5},{8,10},{10,8},{12,... | collective-permute-start | bytes 1572872 | tf_op jit(solution)/shard_map/ppermute | solution.py:471
  391.6 46.0 %collective-permute-start.30 = (bf16[1,2048,128]{2,1,0:T(8,128)(2,1)}, bf16[1,2048,128]{2,1,0:T(8,128)(2,1)}, u32[]{:S(2)}, u32[]{:S(2)}) collective-permute-start(bf16[1,2048,128]{2,1,0:T(8,128)(2,1)} %slice.144), channel_id=1, source_target_pairs={{0,4},{2,6},{4,0},{6,2},{1,5},{3,7},{5,1},{7,3},{8,12},{10,14},{12... | collective-permute-start | bytes 1572872 | tf_op jit(solution)/shard_map/ppermute | solution.py:471
  437.7 120.3 %all-to-all-start.4 = ((bf16[32,4,16,1024]{3,2,1,0:T(8,128)(2,1)}), bf16[32,4,16,1024]{3,2,1,0:T(8,128)(2,1)}, u32[]{:S(2)}, u32[]{:S(2)}) async-start(bf16[32,4,16,1024]{3,2,1,0:T(8,128)(2,1)} %shard_map.107), calls=%async_computation.4 | async-start | bytes 8388608 | tf_op jit(solution)/shard_map/all_to_all | solution.py:630
  443.2 80.7 %collective-permute-start.35 = (bf16[32,64,512]{2,1,0:T(8,128)(2,1)S(1)}, bf16[32,64,512]{2,1,0:T(8,128)(2,1)S(1)}, u32[]{:S(2)}, u32[]{:S(2)}) collective-permute-start(bf16[32,64,512]{2,1,0:T(8,128)(2,1)S(1)} %all-to-all-done.3.refs_0_), channel_id=1, source_target_pairs={{0,1},{1,0},{2,3},{3,2},{4,5},{5,4},{6,7},{7,6},{8,9},{9,8},{10,11... | collective-permute-start | bytes 6291464 | tf_op jit(solution)/shard_map/ppermute | solution.py:475
  445.0 59.5 %collective-permute-start.37 = (bf16[2,2048,128]{2,1,0:T(8,128)(2,1)S(1)}, bf16[2,2048,128]{2,1,0:T(8,128)(2,1)S(1)}, u32[]{:S(2)}, u32[]{:S(2)}) collective-permute-start(bf16[2,2048,128]{2,1,0:T(8,128)(2,1)S(1)} %bitcast.101), channel_id=1, source_target_pairs={{0,4},{2,6},{4,0},{6,2},{1,5},{3,7},{5,1},{7,3},{8,12},{10,14},{12... | collective-permute-start | bytes 3145736 | tf_op jit(solution)/shard_map/ppermute | solution.py:471
  446.3 59.9 %collective-permute-start.36 = (bf16[2,2048,128]{2,1,0:T(8,128)(2,1)S(1)}, bf16[2,2048,128]{2,1,0:T(8,128)(2,1)S(1)}, u32[]{:S(2)}, u32[]{:S(2)}) collective-permute-start(bf16[2,2048,128]{2,1,0:T(8,128)(2,1)S(1)} %bitcast.102), channel_id=1, source_target_pairs={{0,2},{2,0},{4,6},{6,4},{1,3},{3,1},{5,7},{7,5},{8,10},{10,8},{12,... | collective-permute-start | bytes 3145736 | tf_op jit(solution)/shard_map/ppermute | solution.py:471
  449.6 74.2 %collective-permute-start.41 = (bf16[1,2048,128]{2,1,0:T(8,128)(2,1)S(1)}, bf16[1,2048,128]{2,1,0:T(8,128)(2,1)S(1)}, u32[]{:S(2)}, u32[]{:S(2)}) collective-permute-start(bf16[1,2048,128]{2,1,0:T(8,128)(2,1)S(1)} %slice.150), channel_id=1, source_target_pairs={{0,2},{2,0},{4,6},{6,4},{1,3},{3,1},{5,7},{7,5},{8,10},{10,8},{12,... | collective-permute-start | bytes 1572872 | tf_op jit(solution)/shard_map/ppermute | solution.py:471
  450.0 73.9 %collective-permute-start.40 = (bf16[1,2048,128]{2,1,0:T(8,128)(2,1)S(1)}, bf16[1,2048,128]{2,1,0:T(8,128)(2,1)S(1)}, u32[]{:S(2)}, u32[]{:S(2)}) collective-permute-start(bf16[1,2048,128]{2,1,0:T(8,128)(2,1)S(1)} %slice.149), channel_id=1, source_target_pairs={{0,4},{2,6},{4,0},{6,2},{1,5},{3,7},{5,1},{7,3},{8,12},{10,14},{12... | collective-permute-start | bytes 1572872 | tf_op jit(solution)/shard_map/ppermute | solution.py:471
  (53 other events, 1102.8 us)
Sparse Core Ops, SparseCore 0:
  25.0 68.1 all-gather.2
